TPU v7x, 512 devices: a whole 4x4x16 slice. The times are simulated.
512 devices in a mesh: row: 32 (over z_hi, x, core), col: 16 (over z_lo, y).
Axes of the slice: x: 4, y: 4, z: 16 (z_hi: 4, z_lo: 4; z = z_hi * 4 + z_lo), core: 2. Of those that a mesh axis runs over, the one named last changes fastest.
Arguments:
- matrix: float32 [16384, 16384], P('row', 'col'), may hold values from -40 to 40
Outputs:
- rotated: float32 [16384, 16384], P('row', 'col')
All inputs are finite; a program needn't handle non-finite values.
Results may differ from a plain program's by a relative error of at most 0.0003.
Values sent between devices are 32-bit elements; how exact they have to be, the bound alone decides.
A program may use at most 64 MiB of HBM per device.

v0:
```python
import math

import jax
import jax.numpy as jnp
from jax import lax
from jax.sharding import PartitionSpec as P

BLK = 128
RP = 2
INNER = 4
NEWTON = 2


def from_behind(value, axis, steps):
    count = lax.axis_size(axis)
    first, last = (max(0, -steps), min(count, count - steps))
    return lax.ppermute(value, axis, [(source, source + steps) for source in range(first, last)])


def broadcast(block, axis, holder):
    block = jnp.where(lax.axis_index(axis) == holder, block, jnp.zeros_like(block))
    return lax.psum(block, axis)


def product(first, second):
    return jnp.dot(
        first, second, precision=lax.Precision.HIGHEST, preferred_element_type=jnp.float32
    )


def pair_rotation(square):
    order_size = square.shape[0]
    weights = jnp.arange(order_size, dtype=jnp.float32) / (order_size - 1) - 0.5
    stride = 0.25 / math.sqrt(order_size)
    identity = jnp.eye(order_size, dtype=jnp.float32)
    current = square
    rotation = identity
    for inner_step in range(INNER):
        bracket = current * weights[None, :] - weights[:, None] * current
        factor = identity + stride * bracket
        for polish in range(NEWTON):
            factor = 1.5 * factor - 0.5 * product(factor, product(factor.T, factor))
        current = product(factor.T, product(current, factor))
        rotation = product(rotation, factor)
    return rotation


def rotate_rows(data, rotations):
    pair_count = rotations.shape[0]
    grouped = data.reshape(pair_count, -1, data.shape[1])
    turned = jnp.einsum("kpq,kpn->kqn", rotations, grouped, precision=lax.Precision.HIGHEST)
    return turned.reshape(data.shape)


def rotate_cols(data, rotations):
    pair_count = rotations.shape[0]
    grouped = data.reshape(data.shape[0], pair_count, -1)
    turned = jnp.einsum("mkp,kpq->mkq", grouped, rotations, precision=lax.Precision.HIGHEST)
    return turned.reshape(data.shape)


def reorder_rows(data, row_index, row_count):
    local_rows, local_cols = data.shape
    pairs_here = local_rows // (2 * BLK)
    grouped = data.reshape(pairs_here, 2, BLK, local_cols)
    top_blocks = grouped[:, 0]
    bottom_blocks = grouped[:, 1]
    from_before = from_behind(top_blocks[pairs_here - 1], "row", 1)
    from_after = from_behind(bottom_blocks[0], "row", -1)
    is_first = row_index == 0
    is_last = row_index == row_count - 1
    first_top = jnp.where(is_first, top_blocks[0], from_before)
    second_top = jnp.where(is_first, bottom_blocks[0], top_blocks[0])
    new_tops = jnp.concatenate(
        [first_top[None], second_top[None], top_blocks[1 : pairs_here - 1]], axis=0
    )
    last_bottom = jnp.where(is_last, top_blocks[pairs_here - 1], from_after)
    new_bottoms = jnp.concatenate([bottom_blocks[1:], last_bottom[None]], axis=0)
    return jnp.stack([new_tops, new_bottoms], axis=1).reshape(local_rows, local_cols)


def reorder_cols(data, col_index, col_count):
    local_rows, local_cols = data.shape
    pairs_here = local_cols // (2 * BLK)
    grouped = data.reshape(local_rows, pairs_here, 2, BLK)
    top_blocks = grouped[:, :, 0]
    bottom_blocks = grouped[:, :, 1]
    from_before = from_behind(top_blocks[:, pairs_here - 1], "col", 1)
    from_after = from_behind(bottom_blocks[:, 0], "col", -1)
    is_first = col_index == 0
    is_last = col_index == col_count - 1
    first_top = jnp.where(is_first, top_blocks[:, 0], from_before)
    second_top = jnp.where(is_first, bottom_blocks[:, 0], top_blocks[:, 0])
    new_tops = jnp.concatenate(
        [first_top[:, None], second_top[:, None], top_blocks[:, 1 : pairs_here - 1]], axis=1
    )
    last_bottom = jnp.where(is_last, top_blocks[:, pairs_here - 1], from_after)
    new_bottoms = jnp.concatenate([bottom_blocks[:, 1:], last_bottom[:, None]], axis=1)
    return jnp.stack([new_tops, new_bottoms], axis=2).reshape(local_rows, local_cols)


def local(matrix):
    row_count = lax.axis_size("row")
    col_count = lax.axis_size("col")
    row_ratio = row_count // col_count
    row_index = lax.axis_index("row")
    col_index = lax.axis_index("col")
    pair_size = 2 * BLK
    offset_cols = row_index % row_ratio * (RP * pair_size)
    diagonal_band = lax.dynamic_slice_in_dim(matrix, offset_cols, RP * pair_size, 1)
    diagonal_band = diagonal_band.reshape(RP, pair_size, RP, pair_size)
    diagonal = jnp.stack([diagonal_band[j, :, j, :] for j in range(RP)])
    solved = jax.vmap(pair_rotation)(diagonal)
    row_rotations = broadcast(solved, "col", row_index // row_ratio)
    column_rotations = jnp.concatenate(
        [broadcast(solved, "row", row_ratio * col_index + t) for t in range(row_ratio)], axis=0
    )
    turned = rotate_rows(matrix, row_rotations)
    result = rotate_cols(turned, column_rotations)
    result = reorder_rows(result, row_index, row_count)
    return reorder_cols(result, col_index, col_count)


def solution(mesh):
    in_specs = (P("row", "col"),)
    out_specs = P("row", "col")
    return jax.shard_map(local, mesh=mesh, in_specs=in_specs, out_specs=out_specs, check_vma=False)
```

profile of v0, /device:TPU:39, one launch (start us, length us, event | category | flops | bytes accessed | tf_op | source)
XLA Modules:
  0.0 668.5 jit_solution(13759649115637380099)
XLA Ops:
  6.6 1.5 copy-done
  8.1 1.1 constant_dynamic-slice_fusion
  9.2 2.9 reshape.53
  12.0 1.6 fusion.73
  13.7 1.2 fusion.21
  15.0 0.8 fusion.12
  15.8 1.1 fusion.74
  16.8 0.7 fusion.11
  17.5 0.7 fusion.17
  18.2 1.2 fusion.56
  19.4 1.0 fusion.75
  20.5 1.2 fusion.18
  21.7 0.8 fusion.10
  22.5 1.1 fusion.76
  23.6 0.7 fusion.9
  24.3 0.7 fusion.78
  24.9 1.2 fusion.79
  26.1 1.2 fusion.19
  27.4 0.8 fusion.8
  28.2 1.1 fusion.80
  29.2 0.7 fusion.7
  29.9 0.7 fusion.82
  30.6 1.1 fusion.83
  31.7 1.2 fusion.20
  32.9 0.8 fusion.6
  33.7 1.1 fusion.84
  34.8 0.7 fusion.5
  35.5 0.7 fusion.77
  36.1 0.7 fusion.81
  36.8 1.9 broadcast_select_fusion.2
  39.0 0.5 all-reduce.6.cloned.1.call-update
  39.5 159.0 %all-reduce.4.cloned.1.call-done = f32[2,256,256]{2,1,0:T(8,128)} async-done(((f32[2,256,256]{2,1,0:T(8,128)}), f32[2,256,256]{2,1,0:T(8,128)}) %all-reduce.4.cloned.1.call-update) | async-done | bytes 524304 | tf_op jit(solution)/shard_map/psum | solution.py:22
  198.4 4.2 fusion.85
  202.6 3.2 reshape_reshape.9
  205.8 361.5 %all-reduce.6.cloned.1.call-done = (f32[2,256,256]{2,1,0:T(8,128)}, f32[2,256,256]{2,1,0:T(8,128)}) async-done(((f32[2,256,256]{2,1,0:T(8,128)}, f32[2,256,256]{2,1,0:T(8,128)}), (f32[2,256,256]{2,1,0:T(8,128)}, f32[2,256,256]{2,1,0:T(8,128)})) %all-reduce.6.cloned.1.call-update) | async-done | bytes 1048592 | tf_op jit(solution)/shard_map/psum | solution.py:22
  567.3 6.8 %fusion.2 = f32[512,4,256]{0,2,1:T(8,128)} fusion(f32[512,4,256]{2,1,0:T(4,128)} %reshape_reshape.9, f32[2,256,256]{2,1,0:T(8,128)} %get-tuple-element.5, f32[2,256,256]{2,1,0:T(8,128)} %get-tuple-element.6), kind=kOutput, calls=%fused_computation.4 | convolution fusion | flops 1610874880 | bytes 5242880 | tf_op jit(solution)/shard_map/mkp,kpq->mkq/dot_general | solution.py:58
  574.1 3.5 reshape_reshape.10
  577.6 5.1 fusion.71
  582.7 0.3 copy.77
  583.0 7.0 %collective-permute-start = (f32[128,1024]{1,0:T(8,128)S(1)}, f32[128,1024]{1,0:T(8,128)}, u32[]{:S(2)}, u32[]{:S(2)}) collective-permute-start(f32[128,1024]{1,0:T(8,128)S(1)} %bitcast.105), channel_id=1, source_target_pairs={{0,16},{16,32},{32,48},{48,64},{64,80},{80,96},{96,112},{112,128},... | collective-permute-start | bytes 1572872 | tf_op jit(solution)/shard_map/ppermute | solution.py:17
  590.1 1.2 copy.76
  591.3 1.9 copy.78
  593.3 2.2 collective-permute-start.1
  595.5 0.9 select_bitcast_fusion.1
  596.3 2.0 copy.79
  598.3 3.6 collective-permute-done
  601.9 1.1 fusion.16
  603.0 1.2 maximum_bitcast_fusion
  604.2 25.7 %collective-permute-done.1 = f32[128,1024]{1,0:T(8,128)} collective-permute-done((f32[128,1024]{1,0:T(8,128)}, f32[128,1024]{1,0:T(8,128)}, u32[]{:S(2)}, u32[]{:S(2)}) %collective-permute-start.1) | collective-permute-done | bytes 524320 | tf_op jit(solution)/shard_map/ppermute | solution.py:17
  629.9 1.1 select_bitcast_fusion
  631.1 1.5 pad_maximum_fusion
  632.6 4.0 reshape_reshape.11
  636.6 4.0 fusion.70
  640.8 1.9 collective-permute-start.3
  642.7 0.4 fusion.72
  643.4 0.3 slice.83
  643.7 3.4 collective-permute-start.2
  647.1 0.8 collective-permute-done.3
  647.9 0.5 maximum_bitcast_fusion.3
  648.4 4.5 collective-permute-done.2
  652.9 0.7 maximum_bitcast_fusion.2
  653.7 1.8 pad_maximum_fusion.1
  655.5 2.9 copy.59
  658.4 2.9 copy.60
  (17 shorter events, 1.0 us)
Async XLA Ops:
  6.5 1.6 copy-start
  6.5 191.9 %all-reduce.4.cloned.1.call-start = ((), (), s32[]{:S(2)}) async-start(), calls=%async_computation | async-start | bytes 1048576 | tf_op jit(solution)/shard_map/psum | solution.py:22
  32.9 2.6 copy-start.1
  38.7 528.6 %all-reduce.6.cloned.1.call-start = ((), (), s32[]{:S(2)}) async-start(), calls=%async_computation.1 | async-start | bytes 2097152 | tf_op jit(solution)/shard_map/psum | solution.py:22
  583.0 18.9 %collective-permute-start = (f32[128,1024]{1,0:T(8,128)S(1)}, f32[128,1024]{1,0:T(8,128)}, u32[]{:S(2)}, u32[]{:S(2)}) collective-permute-start(f32[128,1024]{1,0:T(8,128)S(1)} %bitcast.105), channel_id=1, source_target_pairs={{0,16},{16,32},{32,48},{48,64},{64,80},{80,96},{96,112},{112,128},... | collective-permute-start | bytes 1572872 | tf_op jit(solution)/shard_map/ppermute | solution.py:17
  593.3 36.6 %collective-permute-start.1 = (f32[128,1024]{1,0:T(8,128)}, f32[128,1024]{1,0:T(8,128)}, u32[]{:S(2)}, u32[]{:S(2)}) collective-permute-start(f32[128,1024]{1,0:T(8,128)} %bitcast.106), channel_id=1, source_target_pairs={{16,0},{32,16},{48,32},{64,48},{80,64},{96,80},{112,96},{128,112},... | collective-permute-start | bytes 1572872 | tf_op jit(solution)/shard_map/ppermute | solution.py:17
  603.0 28.0 %copy-start.2 = (f32[1,1,128,1024]{3,2,1,0:T(8,128)S(1)}, f32[1,1,128,1024]{3,2,1,0:T(8,128)}, u32[]{:S(2)}) copy-start(f32[1,1,128,1024]{3,2,1,0:T(8,128)} %copy.79) | copy-start | bytes 1572868
  640.8 7.1 %collective-permute-start.3 = (f32[512,128]{1,0:T(8,128)S(1)}, f32[512,128]{1,0:T(8,128)S(1)}, u32[]{:S(2)}, u32[]{:S(2)}) collective-permute-start(f32[512,128]{1,0:T(8,128)S(1)} %bitcast.109), channel_id=1, source_target_pairs={{1,0},{2,1},{3,2},{4,3},{5,4},{6,5},{7,6},{8,7},{9,8},{10,9},{11,1... | collective-permute-start | bytes 786440 | tf_op jit(solution)/shard_map/ppermute | solution.py:17
  643.7 9.2 %collective-permute-start.2 = (f32[512,128]{1,0:T(8,128)S(1)}, f32[512,128]{1,0:T(8,128)S(1)}, u32[]{:S(2)}, u32[]{:S(2)}) collective-permute-start(f32[512,128]{1,0:T(8,128)S(1)} %bitcast.111), channel_id=1, source_target_pairs={{0,1},{1,2},{2,3},{3,4},{4,5},{5,6},{6,7},{7,8},{8,9},{9,10},{10,1... | collective-permute-start | bytes 786440 | tf_op jit(solution)/shard_map/ppermute | solution.py:17
Sparse Core Ops, SparseCore 0:
  38.8 159.5 all-reduce.3
  201.6 365.6 all-reduce.5
where the time goes:
time: 678 us; the launch traced here: 669 us
  waiting for transfers between devices  556 us (82%)
  local copies, waits for them, and re-layouts  39.3 us (6%)
  matrix products  35.7 us (5%)
  starting transfers between devices  14.7 us (2%)
  between operations  14.3 us (2%)
  other arithmetic  8.87 us (1%)
    psum x2, waiting for transfers between devices, broadcast(): return lax.psum(block, axis)  520 us
    ppermute x4, waiting for transfers between devices, from_behind(): lax.ppermute(value, axis, [(source, source + steps) for source in range(f...  34.6 us
    dot_general x26, matrix products, product(): jnp.dot(first, second, precision=lax.Precision.HIGHEST, preferred_element...  24.7 us
    ppermute x4, starting transfers between devices, from_behind(): lax.ppermute(value, axis, [(source, source + steps) for source in range(f...  14.5 us
  transfers between devices with their start and end apart: 6, of which 6 were waited for; matrix products, arithmetic and copies ran while one was open for 3% of the time, Pallas kernels for 0%

commit v1 on v0

v1 whole, which is shorter than its diff:
```python
import math

import jax
import jax.numpy as jnp
from jax import lax
from jax.experimental import pallas as pl
from jax.experimental.pallas import tpu as pltpu
from jax.sharding import PartitionSpec as P

MESH = pl.DeviceIdType.MESH
F32 = jnp.float32
BF16 = jnp.bfloat16
BLK = 128
PAIR = 256
INNER = 4
ROWS = 512
COLS = 1024
WIDE = COLS + 2 * PAIR
GROUPS = 16
FOLD = 264


def split(value):
    high = value.astype(BF16)
    return high, (value - high.astype(F32)).astype(BF16)


def product(first, second):
    (first_high, first_low), (second_high, second_low) = first, second
    left = jnp.concatenate([first_high, first_high, first_low], axis=1)
    right = jnp.concatenate([second_high, second_low, second_high], axis=0)
    return jnp.dot(left, right, preferred_element_type=F32)


def pair_rotation(square):
    i = lax.broadcasted_iota(jnp.int32, (PAIR, PAIR), 0)
    j = lax.broadcasted_iota(jnp.int32, (PAIR, PAIR), 1)
    weights = (j - i).astype(F32) * (0.25 / math.sqrt(PAIR) / (PAIR - 1))
    identity = jnp.where(i == j, 1.0, 0.0).astype(F32)
    current = square
    rotation = None
    for inner_step in range(INNER):
        last = inner_step == INNER - 1
        bracket = current * weights
        bracket_s = split(bracket)
        power = product(bracket_s, bracket_s)
        power_s = split(power)
        if not last:
            half = current + product(split(current), bracket_s)
        if rotation is None:
            turned = identity + bracket
        else:
            turned = rotation + product(split(rotation), bracket_s)
        power2 = product(power_s, power_s)
        if not last:
            both = half - product(bracket_s, split(half))
        series = 0.375 * identity + 0.3125 * power + 0.0625 * power2
        polish = split(0.5 * power + product(split(power2), split(series)))
        rotation = turned + product(split(turned), polish)
        if not last:
            half = both + product(split(both), polish)
            current = half + product(polish, split(half))
    return rotation


def fold(square):
    i = lax.broadcasted_iota(jnp.int32, (BLK, BLK), 0)
    j = lax.broadcasted_iota(jnp.int32, (BLK, BLK), 1)
    first, second = square[:BLK, :BLK], square[BLK:, BLK:]
    diagonal = jnp.sum(jnp.where(i == j, second, 0.0), axis=0, keepdims=True)
    return jnp.concatenate(
        [square[:BLK, BLK:], jnp.where(i <= j, first, second), jnp.broadcast_to(diagonal, (8, BLK))], axis=0
    )


def unfold(folded):
    i = lax.broadcasted_iota(jnp.int32, (BLK, BLK), 0)
    j = lax.broadcasted_iota(jnp.int32, (BLK, BLK), 1)
    side = folded[:BLK]
    middle = folded[BLK : 2 * BLK]
    flipped = middle.T
    first = jnp.where(i <= j, middle, flipped)
    second = jnp.where(i > j, middle, jnp.where(i < j, flipped, folded[2 * BLK : 2 * BLK + 1]))
    return jnp.concatenate(
        [jnp.concatenate([first, side], axis=1), jnp.concatenate([side.T, second], axis=1)], axis=0
    )


def choose(cond, yes, no):
    return cond * yes + (1 - cond) * no


def same(a, b):
    return int(a == b) if isinstance(a - b, int) else jnp.where(a == b, 1, 0)


def slot_of(group, member, half):
    step, slot = 0, 0
    for m, h, slot_in, step_in in (
        (0, 0, 2, 0), (1, 0, 4, 0), (2, 0, 6, 0), (3, 0, 0, 1),
        (0, 1, 7, -1), (1, 1, 1, 0), (2, 1, 3, 0), (3, 1, 5, 0),
    ):
        if h == half:
            slot = slot + same(member, m) * slot_in
            step = step + same(member, m) * step_in
    first, last = same(group, 0), same(group, GROUPS - 1)
    if half == 0:
        slot = slot - first * same(member, 0) * 2 + last * same(member, 3) * 7
        step = step - last * same(member, 3)
    else:
        slot = slot - first * same(member, 0) * 5
        step = step + first * same(member, 0)
    return step, slot


def maker_of(group, slot):
    step, member = {0: (-1, 3), 1: (0, 1), 2: (0, 0), 3: (0, 2), 4: (0, 1), 5: (0, 3), 6: (0, 2), 7: (1, 0)}[slot]
    if slot == 0:
        return choose(same(group, 0), 0, step), choose(same(group, 0), 0, member)
    if slot == 7:
        return choose(same(group, GROUPS - 1), 0, step), choose(same(group, GROUPS - 1), 3, member)
    return step, member


class Place:
    def __init__(self, row, col):
        self.row, self.c = row, col
        self.k, self.R = row % 2, row // 2
        self.x, self.zh = self.R % 4, self.R // 4
        self.y, self.zl = self.c % 4, self.c // 4
        self.on_diagonal = same(self.R, self.c)
        self.in_relay = same(self.zh, self.zl)
        self.turn = (self.zh - self.zl + 4) % 4

    def at(self, k=None, x=None, zh=None, y=None, zl=None):
        k = self.k if k is None else k
        x = self.x if x is None else x
        zh = self.zh if zh is None else zh
        y = self.y if y is None else y
        zl = self.zl if zl is None else zl
        return (2 * (4 * zh + x) + k, 4 * zl + y)


def scatter_out(p):
    found = []
    for j in range(2):
        q = 2 * p.k + j
        own = (1 - p.k) * same(p.x, q)
        found.append((j, "col", p.on_diagonal * own, p.on_diagonal * (1 - own), p.at(k=0, x=q)))
        own = p.k * same(p.y, q)
        found.append((j, "row", p.on_diagonal * own, p.on_diagonal * (1 - own), p.at(k=1, y=q)))
    return found


def cross_out(p):
    col = 1 - p.k
    up, down = p.at(zh=(p.zh + 1) % 4), p.at(zh=(p.zh + 3) % 4)
    found = [
        (col * same(p.turn, 0), up, 0),
        (col * same(p.turn, 0), down, 0),
        (col * same(p.turn, 1), up, 1),
        (col * same(p.turn, 3), down, 2),
    ]
    for t in range(1, 4):
        found.append((p.k * p.in_relay, p.at(zl=(p.zl + t) % 4), 0))
    return found


def spread_out(p):
    found = []
    for half in range(2):
        step, slot = slot_of(p.c, p.x, half)
        core = slot % 2
        for t in (2, 1, 3, 0):
            own = (same(step, 0) * (1 - core)) if t == 0 else 0
            device = (2 * (4 * p.zh + (p.x + t) % 4) + core, p.c + step)
            found.append(("col", half, (1 - p.k) * own, (1 - p.k) * (1 - own), device, slot))
        step, slot = slot_of(p.R, p.y, half)
        core = slot // 4
        for t in (2, 1, 3, 0):
            own = (same(step, 0) * core) if t == 0 else 0
            device = (2 * (p.R + step) + core, 4 * p.zl + (p.y + t) % 4)
            found.append(("row", half, p.k * own, p.k * (1 - own), device, slot % 4))
    return found


def outer_out(p):
    forward = p.k
    here = choose(forward, 1 - same(p.R, GROUPS - 1), 1 - same(p.R, 0))
    edge = choose(forward, same(p.x, 3), same(p.x, 0))
    far_x = choose(forward, 0, 3)
    to_zh = (p.zh + choose(forward, 1, 3)) % 4
    next_row = (2 * (p.R + 2 * forward - 1) + 1 - p.k + 32) % 32
    found = []
    for q in range(4):
        relayed = here * edge * (1 - same(far_x, q))
        row = choose(edge, 2 * (4 * to_zh + q) + 1 - p.k, next_row)
        found.append((q, relayed, here * (1 - relayed), (row, p.c)))
    return found


def relay_role(p):
    forward = 1 - p.k
    far_x = choose(forward, 0, 3)
    near_x = choose(forward, 3, 0)
    inside = choose(forward, 1 - same(p.zh, 0), 1 - same(p.zh, 3))
    cond = inside * (1 - same(p.x, far_x))
    from_zh = (p.zh + choose(forward, 3, 1)) % 4
    return cond, p.at(x=far_x), p.at(k=1 - p.k, x=near_x, zh=from_zh)


def edges_out(p):
    found = [(cond, device) for _, _, _, cond, device in scatter_out(p)]
    found += [(cond, device) for cond, device, _ in cross_out(p)]
    found += [(cond, device) for _, _, _, cond, device, _ in spread_out(p)]
    for _, relayed, direct, device in outer_out(p):
        found.append((relayed + direct, device))
    cond, device, _ = relay_role(p)
    found.append((cond, device))
    found.append((1, p.at(k=1 - p.k)))
    found.append((1 - same(p.c, 0), (p.row, p.c - 1)))
    found.append((1 - same(p.c, GROUPS - 1), (p.row, p.c + 1)))
    return found


def edges_in(p):
    col = 1 - p.k
    source = p.at(k=p.x // 2, x=p.y)
    found = [(col * p.in_relay * (1 - same(p.x, p.y) * (1 - p.x // 2)), source)]
    source = p.at(k=p.y // 2, y=p.x)
    found.append((p.k * p.in_relay * (1 - same(p.x, p.y) * (p.y // 2)), source))
    up, down = p.at(zh=(p.zh + 1) % 4), p.at(zh=(p.zh + 3) % 4)
    found.append((col * (same(p.turn, 1) + same(p.turn, 2)), down))
    found.append((col * (same(p.turn, 3) + same(p.turn, 2)), up))
    found.append((p.k * (1 - p.in_relay), p.at(zl=p.zh)))
    for n in range(4):
        step, member = maker_of(p.c, 2 * n)
        step1, member1 = maker_of(p.c, 2 * n + 1)
        step, member = choose(p.k, step1, step), choose(p.k, member1, member)
        own = same(step, 0) * same(member, p.x) * (1 - p.k)
        found.append((1 - own, (2 * (4 * p.zh + member), p.c + step)))
        step, member = maker_of(p.R, n)
        step1, member1 = maker_of(p.R, 4 + n)
        step, member = choose(p.k, step1, step), choose(p.k, member1, member)
        own = same(step, 0) * same(member, p.y) * p.k
        found.append((1 - own, (2 * (p.R + step) + 1, 4 * p.zl + member)))
    forward = 1 - p.k
    here = choose(forward, 1 - same(p.R, 0), 1 - same(p.R, GROUPS - 1))
    far_x = choose(forward, 0, 3)
    edge = same(p.x, far_x)
    relay, _, start = relay_role(p)
    source_row = (2 * (p.R + 1 - 2 * forward) + 1 - p.k + 32) % 32
    for q in range(4):
        direct = choose(edge, same(far_x, q), 1)
        row = choose(edge, choose(direct, start[0], p.at(x=q)[0]), source_row)
        found.append((here, (row, p.c)))
    found.append((relay, start))
    found.append((1, p.at(k=1 - p.k)))
    found.append((1 - same(p.c, 0), (p.row, p.c - 1)))
    found.append((1 - same(p.c, GROUPS - 1), (p.row, p.c + 1)))
    return found


def here():
    return Place(lax.axis_index("row"), lax.axis_index("col"))


def when(cond, action):
    if isinstance(cond, int):
        if cond:
            action()
    else:
        pl.when(cond == 1)(action)


class Sends:
    def __init__(self, sems):
        self.sems, self.pending = sems, []

    def start(self, cond, source, target, recv_sem, device):
        index = len(self.pending)

        def make():
            return pltpu.make_async_remote_copy(
                src_ref=source,
                dst_ref=target,
                send_sem=self.sems.at[index],
                recv_sem=recv_sem,
                device_id=device,
                device_id_type=MESH,
            )

        self.pending.append((cond, make))
        when(cond, lambda: make().start())

    def finish(self):
        for cond, make in self.pending:
            when(cond, lambda make=make: make().wait_send())


def arrived(ref, sem, cond=1):
    when(cond, lambda: pltpu.make_async_copy(ref, ref, sem).wait())


def travel_kernel(
    m_ref, left_ref, right_ref, outer_ref, inner_ref, jc_ref, jr_ref,
    square, folded, solver_in, out_c, out_r, relay,
    load_sem, send_sem, solver_sem, jc_sem, jr_sem, side_sem, outer_sem, outer_side_sem, inner_sem, relay_sem,
):
    p = here()
    loads = []
    for j in range(2):
        column = pl.multiple_of(p.k * ROWS + j * PAIR, PAIR)
        loads.append(
            pltpu.make_async_copy(
                m_ref.at[pl.ds(j * PAIR, PAIR), pl.ds(column, PAIR)], square.at[j], load_sem.at[j]
            )
        )
        when(p.on_diagonal, loads[j].start)

    barrier = pltpu.get_barrier_semaphore()
    for cond, device in edges_in(p):
        when(
            cond,
            lambda device=device: pl.semaphore_signal(barrier, inc=1, device_id=device, device_id_type=MESH),
        )

    def fold_both():
        for j in range(2):
            loads[j].wait()
            folded[j] = fold(square[j])

    when(p.on_diagonal, fold_both)
    pl.semaphore_wait(barrier, sum(cond for cond, _ in edges_out(p)))

    sends = Sends(send_sem)
    mate = p.at(k=1 - p.k)
    before, after = (p.row, p.c - 1), (p.row, p.c + 1)
    has_before, has_after = 1 - same(p.c, 0), 1 - same(p.c, GROUPS - 1)
    low = pl.multiple_of(p.k * PAIR, PAIR)
    other = pl.multiple_of((1 - p.k) * PAIR, PAIR)

    for j, _, own, cond, device in scatter_out(p):
        sends.start(cond, folded.at[j], solver_in, solver_sem.at[0], device)
        when(own, pltpu.make_async_copy(folded.at[j], solver_in, solver_sem.at[0]).start)

    sends.start(has_before, m_ref.at[:, pl.ds(0, PAIR)], right_ref, side_sem.at[1], before)
    sends.start(has_after, m_ref.at[:, pl.ds(COLS - PAIR, PAIR)], left_ref, side_sem.at[0], after)
    sends.start(1, m_ref.at[pl.ds(other, PAIR)], inner_ref.at[:, pl.ds(PAIR, COLS)], inner_sem.at[0], mate)
    for q, relayed, direct, device in outer_out(p):
        part = m_ref.at[pl.ds(low, PAIR), pl.ds(q * PAIR, PAIR)]
        sends.start(relayed, part, relay, relay_sem.at[0], device)
        sends.start(direct, part, outer_ref.at[:, pl.ds(PAIR + q * PAIR, PAIR)], outer_sem.at[q], device)

    whole = choose(1 - p.k, 1 - same(p.turn, 2), 1)
    halves = 1 - whole
    parts = (pl.ds(0, BLK), pl.ds(BLK, FOLD - BLK))
    arrived(solver_in, solver_sem.at[0], whole)
    for n in range(2):
        arrived(solver_in.at[parts[n]], solver_sem.at[1 + n], halves)
    for cond, device, part in cross_out(p):
        ref = solver_in if part == 0 else solver_in.at[parts[part - 1]]
        sends.start(cond, ref, ref, solver_sem.at[part], device)

    rotation = pair_rotation(unfold(solver_in[...]))

    def keep_columns():
        for half in range(2):
            out_c[half] = rotation[:, half * BLK : (half + 1) * BLK]

    def keep_rows():
        flipped = rotation.T
        for half in range(2):
            out_r[half] = flipped[half * BLK : (half + 1) * BLK]

    when(1 - p.k, keep_columns)
    when(p.k, keep_rows)
    for kind, half, own, cond, device, slot in spread_out(p):
        source, target, sem = (out_c, jc_ref, jc_sem) if kind == "col" else (out_r, jr_ref, jr_sem)
        sends.start(cond, source.at[half], target.at[slot], sem.at[slot], device)
        if not isinstance(own, int) or own:
            when(own, pltpu.make_async_copy(source.at[half], target.at[slot], sem.at[slot]).start)

    relaying, relay_to, relay_from = relay_role(p)
    arrived(relay, relay_sem.at[0], relaying)
    sends.start(
        relaying, relay, outer_ref.at[:, pl.ds(pl.multiple_of(PAIR + p.x * PAIR, PAIR), PAIR)], outer_sem.at[p.x], relay_to
    )

    arrived(left_ref, side_sem.at[0], has_before)
    sends.start(has_before, left_ref.at[pl.ds(other, PAIR)], inner_ref.at[:, pl.ds(0, PAIR)], inner_sem.at[1], mate)
    arrived(right_ref, side_sem.at[1], has_after)
    sends.start(
        has_after, right_ref.at[pl.ds(other, PAIR)], inner_ref.at[:, pl.ds(PAIR + COLS, PAIR)], inner_sem.at[2], mate
    )
    has_outer = choose(p.k, 1 - same(p.R, GROUPS - 1), 1 - same(p.R, 0))
    for q in range(4):
        arrived(outer_ref.at[:, pl.ds(PAIR + q * PAIR, PAIR)], outer_sem.at[q], has_outer)
        if q == 0:
            sends.start(
                has_outer * has_before, outer_ref.at[:, pl.ds(PAIR, PAIR)], outer_ref.at[:, pl.ds(PAIR + COLS, PAIR)],
                outer_side_sem.at[1], before,
            )
    sends.start(
        has_outer * has_after, outer_ref.at[:, pl.ds(COLS, PAIR)], outer_ref.at[:, pl.ds(0, PAIR)],
        outer_side_sem.at[0], after,
    )

    for n in range(4):
        slot = 2 * n + p.k
        arrived(jc_ref.at[slot], jc_sem.at[slot])
        sends.start(1, jc_ref.at[slot], jc_ref.at[slot], jc_sem.at[slot], mate)
    for n in range(4):
        arrived(jc_ref.at[2 * n + 1 - p.k], jc_sem.at[2 * n + 1 - p.k])
        arrived(jr_ref.at[n], jr_sem.at[n])

    arrived(inner_ref.at[:, pl.ds(PAIR, COLS)], inner_sem.at[0])
    arrived(inner_ref.at[:, pl.ds(0, PAIR)], inner_sem.at[1], has_before)
    arrived(inner_ref.at[:, pl.ds(PAIR + COLS, PAIR)], inner_sem.at[2], has_after)
    arrived(outer_ref.at[:, pl.ds(0, PAIR)], outer_side_sem.at[0], has_outer * has_before)
    arrived(outer_ref.at[:, pl.ds(PAIR + COLS, PAIR)], outer_side_sem.at[1], has_outer * has_after)
    sends.finish()


def travel(matrix):
    any_spec = pl.BlockSpec(memory_space=pl.ANY)
    shapes = [(ROWS, PAIR), (ROWS, PAIR), (PAIR, WIDE), (PAIR, WIDE), (8, PAIR, BLK), (4, BLK, PAIR)]
    return pl.pallas_call(
        travel_kernel,
        out_shape=[jax.ShapeDtypeStruct(shape, F32) for shape in shapes],
        in_specs=[any_spec],
        out_specs=[any_spec] * len(shapes),
        scratch_shapes=[
            pltpu.VMEM((2, PAIR, PAIR), F32),
            pltpu.VMEM((2, FOLD, BLK), F32),
            pltpu.VMEM((FOLD, BLK), F32),
            pltpu.VMEM((2, PAIR, BLK), F32),
            pltpu.VMEM((2, BLK, PAIR), F32),
            pltpu.VMEM((PAIR, PAIR), F32),
            pltpu.SemaphoreType.DMA((2,)),
            pltpu.SemaphoreType.DMA((64,)),
            pltpu.SemaphoreType.DMA((3,)),
            pltpu.SemaphoreType.DMA((8,)),
            pltpu.SemaphoreType.DMA((4,)),
            pltpu.SemaphoreType.DMA((2,)),
            pltpu.SemaphoreType.DMA((4,)),
            pltpu.SemaphoreType.DMA((2,)),
            pltpu.SemaphoreType.DMA((3,)),
            pltpu.SemaphoreType.DMA((1,)),
        ],
        compiler_params=pltpu.CompilerParams(
            collective_id=1, has_side_effects=True, vmem_limit_bytes=32 * 1024 * 1024
        ),
        cost_estimate=pl.CostEstimate(flops=10**9, bytes_accessed=10**7, transcendentals=0),
        name="travel",
    )(matrix)


SLOTS = (((0,), 0), ((1, 4), 2), ((2,), 1), ((3, 6), 3), ((5,), 4), ((7,), 5))


def apply_kernel(
    m_ref, left_ref, right_ref, outer_ref, inner_ref, jc_ref, jr_ref, o_ref, raw, jc, jr, half_high, half_low, result,
    raw_sem, j_sem, out_sem,
):
    p = here()
    first_col, last_col = same(p.c, 0), same(p.c, GROUPS - 1)
    first_row, last_row = same(p.row, 0), same(p.row, 2 * GROUPS - 1)
    copies_j = [
        pltpu.make_async_copy(jr_ref, jr, j_sem.at[0]),
        pltpu.make_async_copy(jc_ref, jc, j_sem.at[1]),
    ]
    for copy in copies_j:
        copy.start()
    low, middle, high = pl.ds(0, PAIR), pl.ds(PAIR, COLS), pl.ds(PAIR + COLS, PAIR)

    def own_rows(s, pair, cond):
        rows = pl.ds(pair * PAIR, PAIR)
        when(cond, pltpu.make_async_copy(m_ref.at[rows], raw.at[s, :, middle], raw_sem.at[s, 0]).start)
        when(cond * (1 - first_col), pltpu.make_async_copy(left_ref.at[rows], raw.at[s, :, low], raw_sem.at[s, 1]).start)
        when(cond * (1 - last_col), pltpu.make_async_copy(right_ref.at[rows], raw.at[s, :, high], raw_sem.at[s, 2]).start)
        when(
            cond * first_col,
            pltpu.make_async_copy(m_ref.at[rows, pl.ds(0, PAIR)], raw.at[s, :, low], raw_sem.at[s, 1]).start,
        )
        when(
            cond * last_col,
            pltpu.make_async_copy(m_ref.at[rows, pl.ds(COLS - PAIR, PAIR)], raw.at[s, :, high], raw_sem.at[s, 2]).start,
        )

    def sent_rows(s, ref, cond):
        when(cond, pltpu.make_async_copy(ref.at[:, middle], raw.at[s, :, middle], raw_sem.at[s, 0]).start)
        when(cond * (1 - first_col), pltpu.make_async_copy(ref.at[:, low], raw.at[s, :, low], raw_sem.at[s, 1]).start)
        when(cond * (1 - last_col), pltpu.make_async_copy(ref.at[:, high], raw.at[s, :, high], raw_sem.at[s, 2]).start)
        when(
            cond * first_col,
            pltpu.make_async_copy(ref.at[:, pl.ds(PAIR, PAIR)], raw.at[s, :, low], raw_sem.at[s, 1]).start,
        )
        when(
            cond * last_col,
            pltpu.make_async_copy(ref.at[:, pl.ds(COLS, PAIR)], raw.at[s, :, high], raw_sem.at[s, 2]).start,
        )

    own_rows(1, 1, 1)
    own_rows(2, 0, 1)
    own_rows(0, 0, first_row)
    sent_rows(0, outer_ref, (1 - p.k) * (1 - first_row))
    sent_rows(0, inner_ref, p.k)
    own_rows(3, 1, last_row)
    sent_rows(3, outer_ref, p.k * (1 - last_row))
    sent_rows(3, inner_ref, 1 - p.k)
    copies_j[0].wait()
    for s in (1, 2, 0, 3):
        pltpu.make_async_copy(raw.at[s, :, middle], raw.at[s, :, middle], raw_sem.at[s, 0]).wait()
        pltpu.make_async_copy(raw.at[s, :, low], raw.at[s, :, low], raw_sem.at[s, 1]).wait()
        pltpu.make_async_copy(raw.at[s, :, high], raw.at[s, :, high], raw_sem.at[s, 2]).wait()
        turned = product(split(jr[s]), split(raw[s]))
        turned_high, turned_low = split(turned)
        half_high[s * BLK : (s + 1) * BLK] = turned_high
        half_low[s * BLK : (s + 1) * BLK] = turned_low
    copies_j[1].wait()
    stores = []
    for slots, panel in SLOTS:
        columns = pl.ds(panel * PAIR, PAIR)
        rotation = jc[slots[0]] if len(slots) == 1 else jnp.concatenate([jc[slots[0]], jc[slots[1]]], axis=1)
        turned = product((half_high[:, columns], half_low[:, columns]), split(rotation))
        for n, slot in enumerate(slots):
            result[slot] = turned[:, n * BLK : (n + 1) * BLK]
            store = pltpu.make_async_copy(result.at[slot], o_ref.at[:, pl.ds(slot * BLK, BLK)], out_sem.at[slot])
            store.start()
            stores.append(store)
    for store in stores:
        store.wait()


def apply(matrix, parts):
    any_spec = pl.BlockSpec(memory_space=pl.ANY)
    return pl.pallas_call(
        apply_kernel,
        out_shape=jax.ShapeDtypeStruct((ROWS, COLS), F32),
        in_specs=[any_spec] * 7,
        out_specs=any_spec,
        scratch_shapes=[
            pltpu.VMEM((4, PAIR, WIDE), F32),
            pltpu.VMEM((8, PAIR, BLK), F32),
            pltpu.VMEM((4, BLK, PAIR), F32),
            pltpu.VMEM((ROWS, WIDE), BF16),
            pltpu.VMEM((ROWS, WIDE), BF16),
            pltpu.VMEM((8, ROWS, BLK), F32),
            pltpu.SemaphoreType.DMA((4, 3)),
            pltpu.SemaphoreType.DMA((2,)),
            pltpu.SemaphoreType.DMA((8,)),
        ],
        compiler_params=pltpu.CompilerParams(vmem_limit_bytes=48 * 1024 * 1024),
        cost_estimate=pl.CostEstimate(flops=2 * 10**9, bytes_accessed=10**7, transcendentals=0),
        name="apply",
    )(matrix, *parts)


def local(matrix):
    return apply(matrix, travel(matrix))


def solution(mesh):
    spec = P("row", "col")
    return jax.shard_map(local, mesh=mesh, in_specs=(spec,), out_specs=spec, check_vma=False)
```

time: 678 us -> 134 us (0.20)
  the two profiles are of different devices: /device:TPU:39 before, /device:TPU:57 now
where the time goes in v1:
time: 134 us
  Pallas kernels  132 us (99%)
  local copies, waits for them, and re-layouts  1.59 us (1%)
    pallas_call x1, Pallas kernels, travel(): pl.pallas_call(travel_kernel, out_shape=[jax.ShapeDtypeStruct(shape, F32)...  126 us
    pallas_call x1, Pallas kernels, apply(): pl.pallas_call(apply_kernel, out_shape=jax.ShapeDtypeStruct((ROWS, COLS),...  5.88 us

profile of v1, /device:TPU:57, one launch (start us, length us, event | category | flops | bytes accessed | tf_op | source)
XLA Modules:
  0.0 134.0 jit_solution(2026992687121745533)
XLA Ops:
  0.0 0.0 copy-start
  0.0 1.6 %copy-done = f32[512,1024]{1,0:T(8,128)S(1)} copy-done((f32[512,1024]{1,0:T(8,128)S(1)}, f32[512,1024]{1,0:T(8,128)}, u32[]{:S(2)}) %copy-start) | copy-done | bytes 2097176
  1.6 126.5 %travel.1 = (f32[512,256]{1,0:T(8,128)S(1)}, f32[512,256]{1,0:T(8,128)S(1)}, f32[256,1536]{1,0:T(8,128)S(1)}, f32[256,1536]{1,0:T(8,128)S(1)}, f32[8,256,128]{2,1,0:T(8,128)S(1)}, /*index=5*/f32[4,128,256]{2,1,0:T(8,128)S(1)}) custom-call(f32[512,1024]{1,0:T(8,128)S(1)} %copy-done), custom_call_target="tpu_custom_call" | custom-call | flops 1000000000 | bytes 10000000 | tf_op jit(solution)/shard_map/travel/pallas_call | solution.py:428
  128.1 5.9 %apply.1 = f32[512,1024]{1,0:T(8,128)} custom-call(f32[512,1024]{1,0:T(8,128)} %m_ref.3, f32[512,256]{1,0:T(8,128)S(1)} %get-tuple-element.11.left_ref, f32[512,256]{1,0:T(8,128)S(1)} %get-tuple-element.12.right_ref, f32[256,1536]{1,0:T(8,128)S(1)} %get-tuple-element.13.outer_ref, f32[256,1536]{1,0:T(8,128)S(1)} %get-tuple-element.14.inner_ref, ...), custom_call_target="tpu_custom_call" | custom-call | flops 2000000000 | bytes 10000000 | tf_op jit(solution)/shard_map/apply/pallas_call | solution.py:538
Async XLA Ops:
  0.0 1.6 %copy-start = (f32[512,1024]{1,0:T(8,128)S(1)}, f32[512,1024]{1,0:T(8,128)}, u32[]{:S(2)}) copy-start(f32[512,1024]{1,0:T(8,128)} %m_ref.3) | copy-start | bytes 6291460

commit v2 on v1

--- a/solution.py
+++ b/solution.py
@@ -170,49 +170,61 @@
     found = []
     for half in range(2):
         step, slot = slot_of(p.c, p.x, half)
-        core = slot % 2
+        core, stays = slot % 2, same(step, 0)
+        found.append(("col", half, 0, (1 - p.k) * (1 - stays), (2 * p.R + core, p.c + step), slot))
         for t in (2, 1, 3, 0):
-            own = (same(step, 0) * (1 - core)) if t == 0 else 0
-            device = (2 * (4 * p.zh + (p.x + t) % 4) + core, p.c + step)
-            found.append(("col", half, (1 - p.k) * own, (1 - p.k) * (1 - own), device, slot))
+            own = 1 - core if t == 0 else 0
+            device = p.at(k=core, x=(p.x + t) % 4)
+            found.append(("col", half, (1 - p.k) * stays * own, (1 - p.k) * stays * (1 - own), device, slot))
         step, slot = slot_of(p.R, p.y, half)
-        core = slot // 4
+        core, stays = slot // 4, same(step, 0)
+        found.append(("row", half, 0, p.k * (1 - stays), (2 * (p.R + step) + core, p.c), slot % 4))
         for t in (2, 1, 3, 0):
-            own = (same(step, 0) * core) if t == 0 else 0
-            device = (2 * (p.R + step) + core, 4 * p.zl + (p.y + t) % 4)
-            found.append(("row", half, p.k * own, p.k * (1 - own), device, slot % 4))
+            own = core if t == 0 else 0
+            device = p.at(k=core, y=(p.y + t) % 4)
+            found.append(("row", half, p.k * stays * own, p.k * stays * (1 - own), device, slot % 4))
+    return found
+
+
+def hub_out(p):
+    first, last = same(p.c, 0), same(p.c, GROUPS - 1)
+    cond = choose(p.k, same(p.x, 0) * (1 - last), same(p.x, 3) * (1 - first))
+    found = [("col", cond, 7 * p.k, [p.at(x=(p.x + t) % 4) for t in (2, 1, 3)])]
+    first, last = same(p.R, 0), same(p.R, GROUPS - 1)
+    cond = choose(p.k, same(p.y, 0) * (1 - last), same(p.y, 3) * (1 - first))
+    found.append(("row", cond, 3 * p.k, [p.at(y=(p.y + t) % 4) for t in (2, 1, 3)]))
     return found
 
 
 def outer_out(p):
     forward = p.k
     here = choose(forward, 1 - same(p.R, GROUPS - 1), 1 - same(p.R, 0))
-    edge = choose(forward, same(p.x, 3), same(p.x, 0))
-    far_x = choose(forward, 0, 3)
-    to_zh = (p.zh + choose(forward, 1, 3)) % 4
+    own_x = choose(forward, 3, 0)
+    edge = same(p.x, own_x)
     next_row = (2 * (p.R + 2 * forward - 1) + 1 - p.k + 32) % 32
     found = []
     for q in range(4):
-        relayed = here * edge * (1 - same(far_x, q))
-        row = choose(edge, 2 * (4 * to_zh + q) + 1 - p.k, next_row)
+        relayed = here * edge * (1 - same(own_x, q))
+        row = choose(relayed, p.at(x=q)[0], next_row)
         found.append((q, relayed, here * (1 - relayed), (row, p.c)))
     return found
 
 
 def relay_role(p):
-    forward = 1 - p.k
-    far_x = choose(forward, 0, 3)
-    near_x = choose(forward, 3, 0)
-    inside = choose(forward, 1 - same(p.zh, 0), 1 - same(p.zh, 3))
-    cond = inside * (1 - same(p.x, far_x))
-    from_zh = (p.zh + choose(forward, 3, 1)) % 4
-    return cond, p.at(x=far_x), p.at(k=1 - p.k, x=near_x, zh=from_zh)
+    forward = p.k
+    own_x = choose(forward, 3, 0)
+    inside = choose(forward, 1 - same(p.zh, 3), 1 - same(p.zh, 0))
+    cond = inside * (1 - same(p.x, own_x))
+    to_zh = (p.zh + choose(forward, 1, 3)) % 4
+    return cond, p.at(k=1 - p.k, x=3 - own_x, zh=to_zh), p.at(x=own_x)
 
 
 def edges_out(p):
     found = [(cond, device) for _, _, _, cond, device in scatter_out(p)]
     found += [(cond, device) for cond, device, _ in cross_out(p)]
     found += [(cond, device) for _, _, _, cond, device, _ in spread_out(p)]
+    for _, cond, _, devices in hub_out(p):
+        found += [(cond, device) for device in devices]
     for _, relayed, direct, device in outer_out(p):
         found.append((relayed + direct, device))
     cond, device, _ = relay_role(p)
@@ -237,23 +249,24 @@
         step, member = maker_of(p.c, 2 * n)
         step1, member1 = maker_of(p.c, 2 * n + 1)
         step, member = choose(p.k, step1, step), choose(p.k, member1, member)
-        own = same(step, 0) * same(member, p.x) * (1 - p.k)
-        found.append((1 - own, (2 * (4 * p.zh + member), p.c + step)))
+        stays, own = same(step, 0), same(member, p.x)
+        core = choose(stays, 0, choose(own, 0, p.k))
+        found.append((1 - stays * own * (1 - p.k), (2 * (4 * p.zh + member) + core, p.c + own * step)))
         step, member = maker_of(p.R, n)
         step1, member1 = maker_of(p.R, 4 + n)
         step, member = choose(p.k, step1, step), choose(p.k, member1, member)
-        own = same(step, 0) * same(member, p.y) * p.k
-        found.append((1 - own, (2 * (p.R + step) + 1, 4 * p.zl + member)))
+        stays, own = same(step, 0), same(member, p.y)
+        core = choose(stays, 1, choose(own, 1, p.k))
+        found.append((1 - stays * own * p.k, (2 * (p.R + own * step) + core, 4 * p.zl + member)))
     forward = 1 - p.k
     here = choose(forward, 1 - same(p.R, 0), 1 - same(p.R, GROUPS - 1))
-    far_x = choose(forward, 0, 3)
-    edge = same(p.x, far_x)
+    edge = same(p.x, choose(forward, 0, 3))
+    source_row = (2 * (p.R + 1 - 2 * forward) + 1 - p.k + 32) % 32
+    source_zh = source_row // 8
+    for q in range(4):
+        row = choose(edge, 8 * source_zh + 2 * q + 1 - p.k, source_row)
+        found.append((here, (row, p.c)))
     relay, _, start = relay_role(p)
-    source_row = (2 * (p.R + 1 - 2 * forward) + 1 - p.k + 32) % 32
-    for q in range(4):
-        direct = choose(edge, same(far_x, q), 1)
-        row = choose(edge, choose(direct, start[0], p.at(x=q)[0]), source_row)
-        found.append((here, (row, p.c)))
     found.append((relay, start))
     found.append((1, p.at(k=1 - p.k)))
     found.append((1 - same(p.c, 0), (p.row, p.c - 1)))
@@ -362,6 +375,12 @@
         ref = solver_in if part == 0 else solver_in.at[parts[part - 1]]
         sends.start(cond, ref, ref, solver_sem.at[part], device)
 
+    relaying, relay_to, _ = relay_role(p)
+    arrived(relay, relay_sem.at[0], relaying)
+    sends.start(
+        relaying, relay, outer_ref.at[:, pl.ds(pl.multiple_of(PAIR + p.x * PAIR, PAIR), PAIR)], outer_sem.at[p.x], relay_to
+    )
+
     rotation = pair_rotation(unfold(solver_in[...]))
 
     def keep_columns():
@@ -378,14 +397,15 @@
     for kind, half, own, cond, device, slot in spread_out(p):
         source, target, sem = (out_c, jc_ref, jc_sem) if kind == "col" else (out_r, jr_ref, jr_sem)
         sends.start(cond, source.at[half], target.at[slot], sem.at[slot], device)
-        if not isinstance(own, int) or own:
+        if not isinstance(own, int):
             when(own, pltpu.make_async_copy(source.at[half], target.at[slot], sem.at[slot]).start)
 
-    relaying, relay_to, relay_from = relay_role(p)
-    arrived(relay, relay_sem.at[0], relaying)
-    sends.start(
-        relaying, relay, outer_ref.at[:, pl.ds(pl.multiple_of(PAIR + p.x * PAIR, PAIR), PAIR)], outer_sem.at[p.x], relay_to
-    )
+    (_, hub, _, _), (_, hub_r, _, _) = hub_out(p)
+    for kind, cond, slot, devices in hub_out(p):
+        target, sem = (jc_ref, jc_sem) if kind == "col" else (jr_ref, jr_sem)
+        arrived(target.at[slot], sem.at[slot], cond)
+        for device in devices:
+            sends.start(cond, target.at[slot], target.at[slot], sem.at[slot], device)
 
     arrived(left_ref, side_sem.at[0], has_before)
     sends.start(has_before, left_ref.at[pl.ds(other, PAIR)], inner_ref.at[:, pl.ds(0, PAIR)], inner_sem.at[1], mate)
@@ -408,11 +428,11 @@
 
     for n in range(4):
         slot = 2 * n + p.k
-        arrived(jc_ref.at[slot], jc_sem.at[slot])
+        arrived(jc_ref.at[slot], jc_sem.at[slot], 1 - hub * same(slot, 7 * p.k))
         sends.start(1, jc_ref.at[slot], jc_ref.at[slot], jc_sem.at[slot], mate)
     for n in range(4):
         arrived(jc_ref.at[2 * n + 1 - p.k], jc_sem.at[2 * n + 1 - p.k])
-        arrived(jr_ref.at[n], jr_sem.at[n])
+        arrived(jr_ref.at[n], jr_sem.at[n], 1 - hub_r * same(n, 3 * p.k))
 
     arrived(inner_ref.at[:, pl.ds(PAIR, COLS)], inner_sem.at[0])
     arrived(inner_ref.at[:, pl.ds(0, PAIR)], inner_sem.at[1], has_before)
@@ -423,7 +443,7 @@
 
 
 def travel(matrix):
-    any_spec = pl.BlockSpec(memory_space=pl.ANY)
+    any_spec = pl.BlockSpec(memory_space=pltpu.HBM)
     shapes = [(ROWS, PAIR), (ROWS, PAIR), (PAIR, WIDE), (PAIR, WIDE), (8, PAIR, BLK), (4, BLK, PAIR)]
     return pl.pallas_call(
         travel_kernel,
@@ -438,7 +458,7 @@
             pltpu.VMEM((2, BLK, PAIR), F32),
             pltpu.VMEM((PAIR, PAIR), F32),
             pltpu.SemaphoreType.DMA((2,)),
-            pltpu.SemaphoreType.DMA((64,)),
+            pltpu.SemaphoreType.DMA((80,)),
             pltpu.SemaphoreType.DMA((3,)),
             pltpu.SemaphoreType.DMA((8,)),
             pltpu.SemaphoreType.DMA((4,)),
@@ -534,7 +554,7 @@
 
 
 def apply(matrix, parts):
-    any_spec = pl.BlockSpec(memory_space=pl.ANY)
+    any_spec = pl.BlockSpec(memory_space=pltpu.HBM)
     return pl.pallas_call(
         apply_kernel,
         out_shape=jax.ShapeDtypeStruct((ROWS, COLS), F32),

time: 134 us -> 80.9 us (0.60)
  the two profiles are of different devices: /device:TPU:57 before, /device:TPU:65 now
where the time goes in v2:
time: 80.9 us; the launch traced here: 80.8 us
  Pallas kernels  79.2 us (98%)
  local copies, waits for them, and re-layouts  1.59 us (2%)
    pallas_call x1, Pallas kernels, travel(): pl.pallas_call(travel_kernel, out_shape=[jax.ShapeDtypeStruct(shape, F32)...  73.3 us
    pallas_call x1, Pallas kernels, apply(): pl.pallas_call(apply_kernel, out_shape=jax.ShapeDtypeStruct((ROWS, COLS),...  5.87 us

profile of v2, /device:TPU:65, one launch (start us, length us, event | category | flops | bytes accessed | tf_op | source)
XLA Modules:
  0.0 80.8 jit_solution(1059251254514944014)
XLA Ops:
  0.0 0.0 copy-start
  0.0 1.6 %copy-done = f32[512,1024]{1,0:T(8,128)S(1)} copy-done((f32[512,1024]{1,0:T(8,128)S(1)}, f32[512,1024]{1,0:T(8,128)}, u32[]{:S(2)}) %copy-start) | copy-done | bytes 2097176
  1.6 73.3 %travel.1 = (f32[512,256]{1,0:T(8,128)S(1)}, f32[512,256]{1,0:T(8,128)S(1)}, f32[256,1536]{1,0:T(8,128)S(1)}, f32[256,1536]{1,0:T(8,128)S(1)}, f32[8,256,128]{2,1,0:T(8,128)S(1)}, /*index=5*/f32[4,128,256]{2,1,0:T(8,128)S(1)}) custom-call(f32[512,1024]{1,0:T(8,128)S(1)} %copy-done), custom_call_target="tpu_custom_call" | custom-call | flops 1000000000 | bytes 10000000 | tf_op jit(solution)/shard_map/travel/pallas_call | solution.py:448
  74.9 5.9 %apply.1 = f32[512,1024]{1,0:T(8,128)} custom-call(f32[512,1024]{1,0:T(8,128)} %m_ref.3, f32[512,256]{1,0:T(8,128)S(1)} %get-tuple-element.11.left_ref, f32[512,256]{1,0:T(8,128)S(1)} %get-tuple-element.12.right_ref, f32[256,1536]{1,0:T(8,128)S(1)} %get-tuple-element.13.outer_ref, f32[256,1536]{1,0:T(8,128)S(1)} %get-tuple-element.14.inner_ref, ...), custom_call_target="tpu_custom_call" | custom-call | flops 2000000000 | bytes 10000000 | tf_op jit(solution)/shard_map/apply/pallas_call | solution.py:558
Async XLA Ops:
  0.0 1.6 %copy-start = (f32[512,1024]{1,0:T(8,128)S(1)}, f32[512,1024]{1,0:T(8,128)}, u32[]{:S(2)}) copy-start(f32[512,1024]{1,0:T(8,128)} %m_ref.3) | copy-start | bytes 6291460

commit v3 on v2

--- a/solution.py
+++ b/solution.py
@@ -130,7 +130,6 @@
         self.y, self.zl = self.c % 4, self.c // 4
         self.on_diagonal = same(self.R, self.c)
         self.in_relay = same(self.zh, self.zl)
-        self.turn = (self.zh - self.zl + 4) % 4
 
     def at(self, k=None, x=None, zh=None, y=None, zl=None):
         k = self.k if k is None else k
@@ -153,16 +152,11 @@
 
 
 def cross_out(p):
-    col = 1 - p.k
-    up, down = p.at(zh=(p.zh + 1) % 4), p.at(zh=(p.zh + 3) % 4)
-    found = [
-        (col * same(p.turn, 0), up, 0),
-        (col * same(p.turn, 0), down, 0),
-        (col * same(p.turn, 1), up, 1),
-        (col * same(p.turn, 3), down, 2),
-    ]
-    for t in range(1, 4):
-        found.append((p.k * p.in_relay, p.at(zl=(p.zl + t) % 4), 0))
+    found = []
+    for t in (2, 1, 3):
+        row = choose(p.k, p.row, p.at(zh=(p.zh + t) % 4)[0])
+        col = choose(p.k, p.at(zl=(p.zl + t) % 4)[1], p.c)
+        found.append((p.in_relay, (row, col)))
     return found
 
 
@@ -219,9 +213,32 @@
     return cond, p.at(k=1 - p.k, x=3 - own_x, zh=to_zh), p.at(x=own_x)
 
 
+def side_out(p):
+    found = []
+    for side in range(2):
+        exists = 1 - same(p.c, 0 if side else GROUPS - 1)
+        own_y = 0 if side else 3
+        crosses = same(p.y, own_y)
+        for q in range(4):
+            relayed = 0 if q == own_y else exists * crosses
+            col = p.c + 1 - 2 * side
+            if q != own_y:
+                col = choose(relayed, p.at(y=q)[1], col)
+            found.append((side, q, relayed, exists * (1 - relayed), (p.row, col)))
+    return found
+
+
+def side_relay(p):
+    found = []
+    for side in range(2):
+        own_y = 0 if side else 3
+        cond = (1 - same(p.zl, 0 if side else 3)) * (1 - same(p.y, own_y))
+        found.append((side, cond, p.at(y=3 - own_y, zl=(p.zl + (3 if side else 1)) % 4), p.at(y=own_y)))
+    return found
+
+
 def edges_out(p):
-    found = [(cond, device) for _, _, _, cond, device in scatter_out(p)]
-    found += [(cond, device) for cond, device, _ in cross_out(p)]
+    found = cross_out(p)
     found += [(cond, device) for _, _, _, cond, device, _ in spread_out(p)]
     for _, cond, _, devices in hub_out(p):
         found += [(cond, device) for device in devices]
@@ -230,21 +247,24 @@
     cond, device, _ = relay_role(p)
     found.append((cond, device))
     found.append((1, p.at(k=1 - p.k)))
-    found.append((1 - same(p.c, 0), (p.row, p.c - 1)))
-    found.append((1 - same(p.c, GROUPS - 1), (p.row, p.c + 1)))
-    return found
+    found += [(relayed + direct, device) for _, _, relayed, direct, device in side_out(p)]
+    found += [(cond, device) for _, cond, device, _ in side_relay(p)]
+    return found
+
+
+def first_edges_out(p):
+    return [(cond, device) for _, _, _, cond, device in scatter_out(p)]
+
+
+def first_edges_in(p):
+    member, source_x, source_y = choose(p.k, p.y, p.x), choose(p.k, p.x, p.y), choose(p.k, p.x, p.y)
+    own = p.on_diagonal * same(p.k, member // 2)
+    return [(p.in_relay * (1 - own), p.at(k=member // 2, x=source_x, y=source_y))]
 
 
 def edges_in(p):
-    col = 1 - p.k
-    source = p.at(k=p.x // 2, x=p.y)
-    found = [(col * p.in_relay * (1 - same(p.x, p.y) * (1 - p.x // 2)), source)]
-    source = p.at(k=p.y // 2, y=p.x)
-    found.append((p.k * p.in_relay * (1 - same(p.x, p.y) * (p.y // 2)), source))
-    up, down = p.at(zh=(p.zh + 1) % 4), p.at(zh=(p.zh + 3) % 4)
-    found.append((col * (same(p.turn, 1) + same(p.turn, 2)), down))
-    found.append((col * (same(p.turn, 3) + same(p.turn, 2)), up))
-    found.append((p.k * (1 - p.in_relay), p.at(zl=p.zh)))
+    source = choose(p.k, p.row, p.at(zh=p.zl)[0]), choose(p.k, p.at(zl=p.zh)[1], p.c)
+    found = [(1 - p.in_relay, source)]
     for n in range(4):
         step, member = maker_of(p.c, 2 * n)
         step1, member1 = maker_of(p.c, 2 * n + 1)
@@ -269,8 +289,13 @@
     relay, _, start = relay_role(p)
     found.append((relay, start))
     found.append((1, p.at(k=1 - p.k)))
-    found.append((1 - same(p.c, 0), (p.row, p.c - 1)))
-    found.append((1 - same(p.c, GROUPS - 1), (p.row, p.c + 1)))
+    for side, cond, _, source in side_relay(p):
+        found.append((cond, source))
+        own_y = 0 if side else 3
+        exists, crosses = 1 - same(p.c, GROUPS - 1 if side else 0), same(p.y, 3 - own_y)
+        for q in range(4):
+            col = choose(crosses, p.at(y=q, zl=(p.zl + (1 if side else 3)) % 4)[1], p.c - 1 + 2 * side)
+            found.append((exists, (p.row, col)))
     return found
 
 
@@ -315,11 +340,18 @@
     when(cond, lambda: pltpu.make_async_copy(ref, ref, sem).wait())
 
 
-def travel_kernel(
-    m_ref, left_ref, right_ref, outer_ref, inner_ref, jc_ref, jr_ref,
-    square, folded, solver_in, out_c, out_r, relay,
-    load_sem, send_sem, solver_sem, jc_sem, jr_sem, side_sem, outer_sem, outer_side_sem, inner_sem, relay_sem,
-):
+def greet(edges_in, edges_out):
+    barrier = pltpu.get_barrier_semaphore()
+    for cond, device in edges_in:
+        when(
+            cond,
+            lambda device=device: pl.semaphore_signal(barrier, inc=1, device_id=device, device_id_type=MESH),
+        )
+    count = sum(cond for cond, _ in edges_out)
+    pl.when(count > 0)(lambda: pl.semaphore_wait(barrier, count))
+
+
+def first_kernel(m_ref, out_ref, square, folded, received, load_sem, send_sem, receive_sem):
     p = here()
     loads = []
     for j in range(2):
@@ -331,21 +363,34 @@
         )
         when(p.on_diagonal, loads[j].start)
 
-    barrier = pltpu.get_barrier_semaphore()
-    for cond, device in edges_in(p):
-        when(
-            cond,
-            lambda device=device: pl.semaphore_signal(barrier, inc=1, device_id=device, device_id_type=MESH),
-        )
-
     def fold_both():
         for j in range(2):
             loads[j].wait()
             folded[j] = fold(square[j])
 
     when(p.on_diagonal, fold_both)
-    pl.semaphore_wait(barrier, sum(cond for cond, _ in edges_out(p)))
-
+    greet(first_edges_in(p), first_edges_out(p))
+    sends = Sends(send_sem)
+    for j, _, own, cond, device in scatter_out(p):
+        sends.start(cond, folded.at[j], received, receive_sem.at[0], device)
+        when(own, pltpu.make_async_copy(folded.at[j], received, receive_sem.at[0]).start)
+
+    def keep():
+        pltpu.make_async_copy(received, received, receive_sem.at[0]).wait()
+        out_ref[...] = received[...]
+
+    when(p.in_relay, keep)
+    when(1 - p.in_relay, lambda: out_ref.__setitem__(..., jnp.zeros((FOLD, BLK), F32)))
+    sends.finish()
+
+
+def travel_kernel(
+    m_ref, first_ref, left_ref, right_ref, outer_ref, inner_ref, jc_ref, jr_ref,
+    solver_in, out_c, out_r, relay, side_pass,
+    send_sem, solver_sem, jc_sem, jr_sem, side_sem, outer_sem, outer_side_sem, inner_sem, relay_sem, side_pass_sem,
+):
+    p = here()
+    greet(edges_in(p), edges_out(p))
     sends = Sends(send_sem)
     mate = p.at(k=1 - p.k)
     before, after = (p.row, p.c - 1), (p.row, p.c + 1)
@@ -353,35 +398,33 @@
     low = pl.multiple_of(p.k * PAIR, PAIR)
     other = pl.multiple_of((1 - p.k) * PAIR, PAIR)
 
-    for j, _, own, cond, device in scatter_out(p):
-        sends.start(cond, folded.at[j], solver_in, solver_sem.at[0], device)
-        when(own, pltpu.make_async_copy(folded.at[j], solver_in, solver_sem.at[0]).start)
-
-    sends.start(has_before, m_ref.at[:, pl.ds(0, PAIR)], right_ref, side_sem.at[1], before)
-    sends.start(has_after, m_ref.at[:, pl.ds(COLS - PAIR, PAIR)], left_ref, side_sem.at[0], after)
+    for cond, device in cross_out(p):
+        sends.start(cond, first_ref, solver_in, solver_sem.at[0], device)
+
+    sides = (left_ref, right_ref)
+    for side, q, relayed, direct, device in side_out(p):
+        part = m_ref.at[pl.ds(q * BLK, BLK), pl.ds(0 if side else COLS - PAIR, PAIR)]
+        if not isinstance(relayed, int):
+            sends.start(relayed, part, side_pass.at[side], side_pass_sem.at[side], device)
+        sends.start(direct, part, sides[side].at[pl.ds(q * BLK, BLK)], side_sem.at[side, q], device)
     sends.start(1, m_ref.at[pl.ds(other, PAIR)], inner_ref.at[:, pl.ds(PAIR, COLS)], inner_sem.at[0], mate)
     for q, relayed, direct, device in outer_out(p):
         part = m_ref.at[pl.ds(low, PAIR), pl.ds(q * PAIR, PAIR)]
         sends.start(relayed, part, relay, relay_sem.at[0], device)
         sends.start(direct, part, outer_ref.at[:, pl.ds(PAIR + q * PAIR, PAIR)], outer_sem.at[q], device)
 
-    whole = choose(1 - p.k, 1 - same(p.turn, 2), 1)
-    halves = 1 - whole
-    parts = (pl.ds(0, BLK), pl.ds(BLK, FOLD - BLK))
-    arrived(solver_in, solver_sem.at[0], whole)
-    for n in range(2):
-        arrived(solver_in.at[parts[n]], solver_sem.at[1 + n], halves)
-    for cond, device, part in cross_out(p):
-        ref = solver_in if part == 0 else solver_in.at[parts[part - 1]]
-        sends.start(cond, ref, ref, solver_sem.at[part], device)
-
+    for side, cond, device, _ in side_relay(p):
+        arrived(side_pass.at[side], side_pass_sem.at[side], cond)
+        part = pl.ds(pl.multiple_of(p.y * BLK, BLK), BLK)
+        sends.start(cond, side_pass.at[side], sides[side].at[part], side_sem.at[side, p.y], device)
     relaying, relay_to, _ = relay_role(p)
     arrived(relay, relay_sem.at[0], relaying)
     sends.start(
         relaying, relay, outer_ref.at[:, pl.ds(pl.multiple_of(PAIR + p.x * PAIR, PAIR), PAIR)], outer_sem.at[p.x], relay_to
     )
 
-    rotation = pair_rotation(unfold(solver_in[...]))
+    arrived(solver_in, solver_sem.at[0], 1 - p.in_relay)
+    rotation = pair_rotation(unfold(jnp.where(p.in_relay == 1, first_ref[...], solver_in[...])))
 
     def keep_columns():
         for half in range(2):
@@ -407,27 +450,34 @@
         for device in devices:
             sends.start(cond, target.at[slot], target.at[slot], sem.at[slot], device)
 
-    arrived(left_ref, side_sem.at[0], has_before)
-    sends.start(has_before, left_ref.at[pl.ds(other, PAIR)], inner_ref.at[:, pl.ds(0, PAIR)], inner_sem.at[1], mate)
-    arrived(right_ref, side_sem.at[1], has_after)
-    sends.start(
-        has_after, right_ref.at[pl.ds(other, PAIR)], inner_ref.at[:, pl.ds(PAIR + COLS, PAIR)], inner_sem.at[2], mate
-    )
     has_outer = choose(p.k, 1 - same(p.R, GROUPS - 1), 1 - same(p.R, 0))
+    sends_on = choose(p.k, 1 - same(p.x, 3), 1 - same(p.x, 0))
+    (_, _, _, next_device), *_ = outer_out(p)
+    ends = (pl.ds(0, PAIR), pl.ds(PAIR + COLS, PAIR))
+    for side, exists, edge_y in ((0, has_before, 0), (1, has_after, 3)):
+        for q in range(4):
+            arrived(sides[side].at[pl.ds(q * BLK, BLK)], side_sem.at[side, q], exists)
+        sends.start(
+            exists, sides[side].at[pl.ds(other, PAIR)], inner_ref.at[:, ends[side]], inner_sem.at[1 + side], mate
+        )
+        sends.start(
+            sends_on * exists * same(p.y, edge_y), sides[side].at[pl.ds(low, PAIR)], outer_ref.at[:, ends[side]],
+            outer_side_sem.at[side], next_device,
+        )
     for q in range(4):
         arrived(outer_ref.at[:, pl.ds(PAIR + q * PAIR, PAIR)], outer_sem.at[q], has_outer)
         if q == 0:
             sends.start(
-                has_outer * has_before, outer_ref.at[:, pl.ds(PAIR, PAIR)], outer_ref.at[:, pl.ds(PAIR + COLS, PAIR)],
-                outer_side_sem.at[1], before,
+                has_outer * has_before * (1 - sends_on * same(p.y, 0)), outer_ref.at[:, pl.ds(PAIR, PAIR)],
+                outer_ref.at[:, ends[1]], outer_side_sem.at[1], before,
             )
     sends.start(
-        has_outer * has_after, outer_ref.at[:, pl.ds(COLS, PAIR)], outer_ref.at[:, pl.ds(0, PAIR)],
-        outer_side_sem.at[0], after,
+        has_outer * has_after * (1 - sends_on * same(p.y, 3)), outer_ref.at[:, pl.ds(COLS, PAIR)],
+        outer_ref.at[:, ends[0]], outer_side_sem.at[0], after,
     )
 
-    for n in range(4):
-        slot = 2 * n + p.k
+    for n in (1, 2, 3, 0):
+        slot = choose(p.k, (1, 3, 5, 7)[n - 1], 2 * n)
         arrived(jc_ref.at[slot], jc_sem.at[slot], 1 - hub * same(slot, 7 * p.k))
         sends.start(1, jc_ref.at[slot], jc_ref.at[slot], jc_sem.at[slot], mate)
     for n in range(4):
@@ -442,38 +492,58 @@
     sends.finish()
 
 
-def travel(matrix):
-    any_spec = pl.BlockSpec(memory_space=pltpu.HBM)
+MIB = 1024 * 1024
+
+
+def first(matrix):
+    return pl.pallas_call(
+        first_kernel,
+        out_shape=jax.ShapeDtypeStruct((FOLD, BLK), F32),
+        in_specs=[pl.BlockSpec(memory_space=pltpu.HBM)],
+        out_specs=pl.BlockSpec(memory_space=pltpu.VMEM),
+        scratch_shapes=[
+            pltpu.VMEM((2, PAIR, PAIR), F32),
+            pltpu.VMEM((2, FOLD, BLK), F32),
+            pltpu.VMEM((FOLD, BLK), F32),
+            pltpu.SemaphoreType.DMA((2,)),
+            pltpu.SemaphoreType.DMA((4,)),
+            pltpu.SemaphoreType.DMA((1,)),
+        ],
+        compiler_params=pltpu.CompilerParams(collective_id=0, has_side_effects=True, vmem_limit_bytes=62 * MIB),
+        cost_estimate=pl.CostEstimate(flops=10**6, bytes_accessed=10**6, transcendentals=0),
+        name="first",
+    )(matrix)
+
+
+def travel(matrix, folded):
+    any_spec = pl.BlockSpec(memory_space=pl.ANY)
     shapes = [(ROWS, PAIR), (ROWS, PAIR), (PAIR, WIDE), (PAIR, WIDE), (8, PAIR, BLK), (4, BLK, PAIR)]
     return pl.pallas_call(
         travel_kernel,
         out_shape=[jax.ShapeDtypeStruct(shape, F32) for shape in shapes],
-        in_specs=[any_spec],
+        in_specs=[pl.BlockSpec(memory_space=pltpu.HBM), pl.BlockSpec(memory_space=pltpu.VMEM)],
         out_specs=[any_spec] * len(shapes),
         scratch_shapes=[
-            pltpu.VMEM((2, PAIR, PAIR), F32),
-            pltpu.VMEM((2, FOLD, BLK), F32),
             pltpu.VMEM((FOLD, BLK), F32),
             pltpu.VMEM((2, PAIR, BLK), F32),
             pltpu.VMEM((2, BLK, PAIR), F32),
             pltpu.VMEM((PAIR, PAIR), F32),
-            pltpu.SemaphoreType.DMA((2,)),
-            pltpu.SemaphoreType.DMA((80,)),
-            pltpu.SemaphoreType.DMA((3,)),
+            pltpu.VMEM((2, BLK, PAIR), F32),
+            pltpu.SemaphoreType.DMA((96,)),
+            pltpu.SemaphoreType.DMA((1,)),
             pltpu.SemaphoreType.DMA((8,)),
             pltpu.SemaphoreType.DMA((4,)),
-            pltpu.SemaphoreType.DMA((2,)),
+            pltpu.SemaphoreType.DMA((2, 4)),
             pltpu.SemaphoreType.DMA((4,)),
             pltpu.SemaphoreType.DMA((2,)),
             pltpu.SemaphoreType.DMA((3,)),
             pltpu.SemaphoreType.DMA((1,)),
+            pltpu.SemaphoreType.DMA((2,)),
         ],
-        compiler_params=pltpu.CompilerParams(
-            collective_id=1, has_side_effects=True, vmem_limit_bytes=32 * 1024 * 1024
-        ),
+        compiler_params=pltpu.CompilerParams(collective_id=1, has_side_effects=True, vmem_limit_bytes=32 * MIB),
         cost_estimate=pl.CostEstimate(flops=10**9, bytes_accessed=10**7, transcendentals=0),
         name="travel",
-    )(matrix)
+    )(matrix, folded)
 
 
 SLOTS = (((0,), 0), ((1, 4), 2), ((2,), 1), ((3, 6), 3), ((5,), 4), ((7,), 5))
@@ -571,14 +641,14 @@
             pltpu.SemaphoreType.DMA((2,)),
             pltpu.SemaphoreType.DMA((8,)),
         ],
-        compiler_params=pltpu.CompilerParams(vmem_limit_bytes=48 * 1024 * 1024),
+        compiler_params=pltpu.CompilerParams(vmem_limit_bytes=48 * MIB),
         cost_estimate=pl.CostEstimate(flops=2 * 10**9, bytes_accessed=10**7, transcendentals=0),
         name="apply",
     )(matrix, *parts)
 
 
 def local(matrix):
-    return apply(matrix, travel(matrix))
+    return apply(matrix, travel(matrix, first(matrix)))
 
 
 def solution(mesh):

time: 80.9 us -> 64.8 us (0.80)
  the two profiles are of different devices: /device:TPU:65 before, /device:TPU:79 now
where the time goes in v3:
time: 64.8 us; the launch traced here: 64.5 us
  Pallas kernels  62 us (96%)
  local copies, waits for them, and re-layouts  2.49 us (4%)
    pallas_call x1, Pallas kernels, travel(): pl.pallas_call(travel_kernel, out_shape=[jax.ShapeDtypeStruct(shape, F32)...  54.6 us
    pallas_call x1, Pallas kernels, apply(): pl.pallas_call(apply_kernel, out_shape=jax.ShapeDtypeStruct((ROWS, COLS),...  5.88 us
    unnamed x4, local copies, waits for them, and re-layouts  2.49 us
    pallas_call x1, Pallas kernels, first(): pl.pallas_call(first_kernel, out_shape=jax.ShapeDtypeStruct((FOLD, BLK),...  1.54 us

profile of v3, /device:TPU:79, one launch (start us, length us, event | category | flops | bytes accessed | tf_op | source)
XLA Modules:
  0.0 64.5 jit_solution(33473087921632880)
XLA Ops:
  0.0 1.5 %first.1.first_ref = f32[264,128]{1,0:T(8,128)} custom-call(f32[512,1024]{1,0:T(8,128)} %m_ref.5), custom_call_target="tpu_custom_call" | custom-call | flops 1000000 | bytes 1000000 | tf_op jit(solution)/shard_map/first/pallas_call | solution.py:499
  1.6 0.0 copy-start
  1.6 1.6 %copy-done = f32[512,1024]{1,0:T(8,128)S(1)} copy-done((f32[512,1024]{1,0:T(8,128)S(1)}, f32[512,1024]{1,0:T(8,128)}, u32[]{:S(2)}) %copy-start) | copy-done | bytes 2097176
  3.1 0.0 copy-start.1
  3.1 0.9 %copy-done.1 = f32[264,128]{1,0:T(8,128)S(1)} copy-done((f32[264,128]{1,0:T(8,128)S(1)}, f32[264,128]{1,0:T(8,128)}, u32[]{:S(2)}) %copy-start.1) | copy-done | bytes 135192
  4.1 54.6 %travel.1 = (f32[512,256]{1,0:T(8,128)S(1)}, f32[512,256]{1,0:T(8,128)S(1)}, f32[256,1536]{1,0:T(8,128)S(1)}, f32[256,1536]{1,0:T(8,128)S(1)}, f32[8,256,128]{2,1,0:T(8,128)S(1)}, /*index=5*/f32[4,128,256]{2,1,0:T(8,128)S(1)}) custom-call(f32[512,1024]{1,0:T(8,128)S(1)} %copy-done, f32[264,128]{1,0:T(8,128)S(1)} %copy-done.1), custom_call_target="tpu_custom_call" | custom-call | flops 1000000000 | bytes 10000000 | tf_op jit(solution)/shard_map/travel/pallas_call | solution.py:521
  58.7 5.9 %apply.1 = f32[512,1024]{1,0:T(8,128)} custom-call(f32[512,1024]{1,0:T(8,128)} %m_ref.5, f32[512,256]{1,0:T(8,128)S(1)} %get-tuple-element.11.left_ref, f32[512,256]{1,0:T(8,128)S(1)} %get-tuple-element.12.right_ref, f32[256,1536]{1,0:T(8,128)S(1)} %get-tuple-element.13.outer_ref, f32[256,1536]{1,0:T(8,128)S(1)} %get-tuple-element.14.inner_ref, ...), custom_call_target="tpu_custom_call" | custom-call | flops 2000000000 | bytes 10000000 | tf_op jit(solution)/shard_map/apply/pallas_call | solution.py:628
Async XLA Ops:
  1.6 1.6 %copy-start = (f32[512,1024]{1,0:T(8,128)S(1)}, f32[512,1024]{1,0:T(8,128)}, u32[]{:S(2)}) copy-start(f32[512,1024]{1,0:T(8,128)} %m_ref.5) | copy-start | bytes 6291460
  3.1 0.9 %copy-start.1 = (f32[264,128]{1,0:T(8,128)S(1)}, f32[264,128]{1,0:T(8,128)}, u32[]{:S(2)}) copy-start(f32[264,128]{1,0:T(8,128)} %first.1.first_ref) | copy-start | bytes 405508

commit v4 on v3

--- a/solution.py
+++ b/solution.py
@@ -443,13 +443,6 @@
         if not isinstance(own, int):
             when(own, pltpu.make_async_copy(source.at[half], target.at[slot], sem.at[slot]).start)
 
-    (_, hub, _, _), (_, hub_r, _, _) = hub_out(p)
-    for kind, cond, slot, devices in hub_out(p):
-        target, sem = (jc_ref, jc_sem) if kind == "col" else (jr_ref, jr_sem)
-        arrived(target.at[slot], sem.at[slot], cond)
-        for device in devices:
-            sends.start(cond, target.at[slot], target.at[slot], sem.at[slot], device)
-
     has_outer = choose(p.k, 1 - same(p.R, GROUPS - 1), 1 - same(p.R, 0))
     sends_on = choose(p.k, 1 - same(p.x, 3), 1 - same(p.x, 0))
     (_, _, _, next_device), *_ = outer_out(p)
@@ -464,17 +457,29 @@
             sends_on * exists * same(p.y, edge_y), sides[side].at[pl.ds(low, PAIR)], outer_ref.at[:, ends[side]],
             outer_side_sem.at[side], next_device,
         )
-    for q in range(4):
-        arrived(outer_ref.at[:, pl.ds(PAIR + q * PAIR, PAIR)], outer_sem.at[q], has_outer)
-        if q == 0:
-            sends.start(
-                has_outer * has_before * (1 - sends_on * same(p.y, 0)), outer_ref.at[:, pl.ds(PAIR, PAIR)],
-                outer_ref.at[:, ends[1]], outer_side_sem.at[1], before,
-            )
-    sends.start(
-        has_outer * has_after * (1 - sends_on * same(p.y, 3)), outer_ref.at[:, pl.ds(COLS, PAIR)],
-        outer_ref.at[:, ends[0]], outer_side_sem.at[0], after,
-    )
+
+    def outer_corners(cond):
+        for q in range(4):
+            arrived(outer_ref.at[:, pl.ds(PAIR + q * PAIR, PAIR)], outer_sem.at[q], cond * has_outer)
+            if q == 0:
+                sends.start(
+                    cond * has_outer * has_before * (1 - sends_on * same(p.y, 0)), outer_ref.at[:, pl.ds(PAIR, PAIR)],
+                    outer_ref.at[:, ends[1]], outer_side_sem.at[1], before,
+                )
+        sends.start(
+            cond * has_outer * has_after * (1 - sends_on * same(p.y, 3)), outer_ref.at[:, pl.ds(COLS, PAIR)],
+            outer_ref.at[:, ends[0]], outer_side_sem.at[0], after,
+        )
+
+    outer_corners(sends_on)
+    (_, hub, _, _), (_, hub_r, _, _) = hub_out(p)
+    for kind, cond, slot, devices in hub_out(p):
+        target, sem = (jc_ref, jc_sem) if kind == "col" else (jr_ref, jr_sem)
+        arrived(target.at[slot], sem.at[slot], cond)
+        for device in devices:
+            sends.start(cond, target.at[slot], target.at[slot], sem.at[slot], device)
+
+    outer_corners(1 - sends_on)
 
     for n in (1, 2, 3, 0):
         slot = choose(p.k, (1, 3, 5, 7)[n - 1], 2 * n)
@@ -498,7 +503,7 @@
 def first(matrix):
     return pl.pallas_call(
         first_kernel,
-        out_shape=jax.ShapeDtypeStruct((FOLD, BLK), F32),
+        out_shape=pltpu.VMEM((FOLD, BLK), F32),
         in_specs=[pl.BlockSpec(memory_space=pltpu.HBM)],
         out_specs=pl.BlockSpec(memory_space=pltpu.VMEM),
         scratch_shapes=[
@@ -520,7 +525,7 @@
     shapes = [(ROWS, PAIR), (ROWS, PAIR), (PAIR, WIDE), (PAIR, WIDE), (8, PAIR, BLK), (4, BLK, PAIR)]
     return pl.pallas_call(
         travel_kernel,
-        out_shape=[jax.ShapeDtypeStruct(shape, F32) for shape in shapes],
+        out_shape=[pltpu.VMEM(shape, F32) for shape in shapes],
         in_specs=[pl.BlockSpec(memory_space=pltpu.HBM), pl.BlockSpec(memory_space=pltpu.VMEM)],
         out_specs=[any_spec] * len(shapes),
         scratch_shapes=[
@@ -529,7 +534,7 @@
             pltpu.VMEM((2, BLK, PAIR), F32),
             pltpu.VMEM((PAIR, PAIR), F32),
             pltpu.VMEM((2, BLK, PAIR), F32),
-            pltpu.SemaphoreType.DMA((96,)),
+            pltpu.SemaphoreType.DMA((112,)),
             pltpu.SemaphoreType.DMA((1,)),
             pltpu.SemaphoreType.DMA((8,)),
             pltpu.SemaphoreType.DMA((4,)),
@@ -604,7 +609,9 @@
         pltpu.make_async_copy(raw.at[s, :, middle], raw.at[s, :, middle], raw_sem.at[s, 0]).wait()
         pltpu.make_async_copy(raw.at[s, :, low], raw.at[s, :, low], raw_sem.at[s, 1]).wait()
         pltpu.make_async_copy(raw.at[s, :, high], raw.at[s, :, high], raw_sem.at[s, 2]).wait()
-        turned = product(split(jr[s]), split(raw[s]))
+        (high_j, low_j), (high_m, low_m) = split(jr[s]), split(raw[s])
+        both = jnp.dot(jnp.concatenate([high_j, low_j], axis=0), high_m, preferred_element_type=F32)
+        turned = both[:BLK] + both[BLK:] + jnp.dot(high_j, low_m, preferred_element_type=F32)
         turned_high, turned_low = split(turned)
         half_high[s * BLK : (s + 1) * BLK] = turned_high
         half_low[s * BLK : (s + 1) * BLK] = turned_low
@@ -612,8 +619,15 @@
     stores = []
     for slots, panel in SLOTS:
         columns = pl.ds(panel * PAIR, PAIR)
-        rotation = jc[slots[0]] if len(slots) == 1 else jnp.concatenate([jc[slots[0]], jc[slots[1]]], axis=1)
-        turned = product((half_high[:, columns], half_low[:, columns]), split(rotation))
+        if len(slots) == 1:
+            high_j, low_j = split(jc[slots[0]])
+            both = jnp.dot(
+                half_high[:, columns], jnp.concatenate([high_j, low_j], axis=1), preferred_element_type=F32
+            )
+            turned = both[:, :BLK] + both[:, BLK:] + jnp.dot(half_low[:, columns], high_j, preferred_element_type=F32)
+        else:
+            rotation = jnp.concatenate([jc[slots[0]], jc[slots[1]]], axis=1)
+            turned = product((half_high[:, columns], half_low[:, columns]), split(rotation))
         for n, slot in enumerate(slots):
             result[slot] = turned[:, n * BLK : (n + 1) * BLK]
             store = pltpu.make_async_copy(result.at[slot], o_ref.at[:, pl.ds(slot * BLK, BLK)], out_sem.at[slot])
@@ -648,6 +662,7 @@
 
 
 def local(matrix):
+    matrix = pltpu.with_memory_space_constraint(matrix, pltpu.HBM)
     return apply(matrix, travel(matrix, first(matrix)))
 
 

time: 64.8 us -> 60.6 us (0.935)
  local copies, waits for them, and re-layouts: 2.49 us -> 0 us
  Pallas kernels: 62 us -> 60.4 us
    unnamed x4 -> x0, local copies, waits for them, and re-layouts: 2.49 us -> none
    pallas_call x2, Pallas kernels: 56.1 us -> 54.9 us  [the longest x1 54 us: travel(): pl.pallas_call(travel_kernel, out_shape=[pltpu.VMEM(shape, F32) for shape...]
where the time goes in v4:
time: 60.6 us; the launch traced here: 60.4 us
  Pallas kernels  60.4 us (100%)
    pallas_call x1, Pallas kernels, travel(): pl.pallas_call(travel_kernel, out_shape=[pltpu.VMEM(shape, F32) for shape...  54 us
    pallas_call x1, Pallas kernels, apply(): pl.pallas_call(apply_kernel, out_shape=jax.ShapeDtypeStruct((ROWS, COLS),...  5.49 us

profile of v4, /device:TPU:79, one launch (start us, length us, event | category | flops | bytes accessed | tf_op | source)
XLA Modules:
  0.0 60.4 jit_solution(1051542468521120090)
XLA Ops:
  0.0 0.9 %first.1.first_ref = f32[264,128]{1,0:T(8,128)S(1)} custom-call(f32[512,1024]{1,0:T(8,128)} %m_ref.5), custom_call_target="tpu_custom_call" | custom-call | flops 1000000 | bytes 1000000 | tf_op jit(solution)/shard_map/first/pallas_call | solution.py:504
  0.9 54.0 %travel.1 = (f32[512,256]{1,0:T(8,128)S(1)}, f32[512,256]{1,0:T(8,128)S(1)}, f32[256,1536]{1,0:T(8,128)S(1)}, f32[256,1536]{1,0:T(8,128)S(1)}, f32[8,256,128]{2,1,0:T(8,128)S(1)}, /*index=5*/f32[4,128,256]{2,1,0:T(8,128)S(1)}) custom-call(f32[512,1024]{1,0:T(8,128)} %m_ref.5, f32[264,128]{1,0:T(8,128)S(1)} %first.1.first_ref), custom_call_target="tpu_custom_call" | custom-call | flops 1000000000 | bytes 10000000 | tf_op jit(solution)/shard_map/travel/pallas_call | solution.py:526
  55.0 5.5 %apply.1 = f32[512,1024]{1,0:T(8,128)} custom-call(f32[512,1024]{1,0:T(8,128)} %m_ref.5, f32[512,256]{1,0:T(8,128)S(1)} %get-tuple-element.11.left_ref, f32[512,256]{1,0:T(8,128)S(1)} %get-tuple-element.12.right_ref, f32[256,1536]{1,0:T(8,128)S(1)} %get-tuple-element.13.outer_ref, f32[256,1536]{1,0:T(8,128)S(1)} %get-tuple-element.14.inner_ref, ...), custom_call_target="tpu_custom_call" | custom-call | flops 2000000000 | bytes 10000000 | tf_op jit(solution)/shard_map/apply/pallas_call | solution.py:642

commit v5 on v4

--- a/solution.py
+++ b/solution.py
@@ -555,67 +555,52 @@
 
 
 def apply_kernel(
-    m_ref, left_ref, right_ref, outer_ref, inner_ref, jc_ref, jr_ref, o_ref, raw, jc, jr, half_high, half_low, result,
-    raw_sem, j_sem, out_sem,
+    m_ref, left_ref, right_ref, outer_ref, inner_ref, jc, jr, o_ref, own, half_high, half_low, result, own_sem, out_sem,
 ):
     p = here()
-    first_col, last_col = same(p.c, 0), same(p.c, GROUPS - 1)
     first_row, last_row = same(p.row, 0), same(p.row, 2 * GROUPS - 1)
-    copies_j = [
-        pltpu.make_async_copy(jr_ref, jr, j_sem.at[0]),
-        pltpu.make_async_copy(jc_ref, jc, j_sem.at[1]),
-    ]
-    for copy in copies_j:
-        copy.start()
+    loads = []
+    for pair in (1, 0):
+        rows = pl.ds(pair * PAIR, PAIR)
+        loads.append(pltpu.make_async_copy(m_ref.at[rows], own.at[rows], own_sem.at[pair]))
+        loads[-1].start()
     low, middle, high = pl.ds(0, PAIR), pl.ds(PAIR, COLS), pl.ds(PAIR + COLS, PAIR)
 
-    def own_rows(s, pair, cond):
+    def turn(s, parts):
+        high_j, low_j = split(jr[s])
+        stacked = jnp.concatenate([high_j, low_j], axis=0)
+        for columns, part in parts:
+            high_m, low_m = split(part())
+            both = jnp.dot(stacked, high_m, preferred_element_type=F32)
+            turned = both[:BLK] + both[BLK:] + jnp.dot(high_j, low_m, preferred_element_type=F32)
+            turned_high, turned_low = split(turned)
+            half_high[s * BLK : (s + 1) * BLK, columns] = turned_high
+            half_low[s * BLK : (s + 1) * BLK, columns] = turned_low
+
+    def own_rows(s, pair):
         rows = pl.ds(pair * PAIR, PAIR)
-        when(cond, pltpu.make_async_copy(m_ref.at[rows], raw.at[s, :, middle], raw_sem.at[s, 0]).start)
-        when(cond * (1 - first_col), pltpu.make_async_copy(left_ref.at[rows], raw.at[s, :, low], raw_sem.at[s, 1]).start)
-        when(cond * (1 - last_col), pltpu.make_async_copy(right_ref.at[rows], raw.at[s, :, high], raw_sem.at[s, 2]).start)
-        when(
-            cond * first_col,
-            pltpu.make_async_copy(m_ref.at[rows, pl.ds(0, PAIR)], raw.at[s, :, low], raw_sem.at[s, 1]).start,
-        )
-        when(
-            cond * last_col,
-            pltpu.make_async_copy(m_ref.at[rows, pl.ds(COLS - PAIR, PAIR)], raw.at[s, :, high], raw_sem.at[s, 2]).start,
-        )
-
-    def sent_rows(s, ref, cond):
-        when(cond, pltpu.make_async_copy(ref.at[:, middle], raw.at[s, :, middle], raw_sem.at[s, 0]).start)
-        when(cond * (1 - first_col), pltpu.make_async_copy(ref.at[:, low], raw.at[s, :, low], raw_sem.at[s, 1]).start)
-        when(cond * (1 - last_col), pltpu.make_async_copy(ref.at[:, high], raw.at[s, :, high], raw_sem.at[s, 2]).start)
-        when(
-            cond * first_col,
-            pltpu.make_async_copy(ref.at[:, pl.ds(PAIR, PAIR)], raw.at[s, :, low], raw_sem.at[s, 1]).start,
-        )
-        when(
-            cond * last_col,
-            pltpu.make_async_copy(ref.at[:, pl.ds(COLS, PAIR)], raw.at[s, :, high], raw_sem.at[s, 2]).start,
-        )
-
-    own_rows(1, 1, 1)
-    own_rows(2, 0, 1)
-    own_rows(0, 0, first_row)
-    sent_rows(0, outer_ref, (1 - p.k) * (1 - first_row))
-    sent_rows(0, inner_ref, p.k)
-    own_rows(3, 1, last_row)
-    sent_rows(3, outer_ref, p.k * (1 - last_row))
-    sent_rows(3, inner_ref, 1 - p.k)
-    copies_j[0].wait()
-    for s in (1, 2, 0, 3):
-        pltpu.make_async_copy(raw.at[s, :, middle], raw.at[s, :, middle], raw_sem.at[s, 0]).wait()
-        pltpu.make_async_copy(raw.at[s, :, low], raw.at[s, :, low], raw_sem.at[s, 1]).wait()
-        pltpu.make_async_copy(raw.at[s, :, high], raw.at[s, :, high], raw_sem.at[s, 2]).wait()
-        (high_j, low_j), (high_m, low_m) = split(jr[s]), split(raw[s])
-        both = jnp.dot(jnp.concatenate([high_j, low_j], axis=0), high_m, preferred_element_type=F32)
-        turned = both[:BLK] + both[BLK:] + jnp.dot(high_j, low_m, preferred_element_type=F32)
-        turned_high, turned_low = split(turned)
-        half_high[s * BLK : (s + 1) * BLK] = turned_high
-        half_low[s * BLK : (s + 1) * BLK] = turned_low
-    copies_j[1].wait()
+        turn(s, ((middle, lambda: own[rows]), (low, lambda: left_ref[rows]), (high, lambda: right_ref[rows])))
+
+    def sent_rows(s, ref):
+        turn(s, ((middle, lambda: ref[:, middle]), (low, lambda: ref[:, low]), (high, lambda: ref[:, high])))
+
+    when((1 - p.k) * (1 - first_row), lambda: sent_rows(0, outer_ref))
+    when(p.k, lambda: sent_rows(0, inner_ref))
+    when(p.k * (1 - last_row), lambda: sent_rows(3, outer_ref))
+    when(1 - p.k, lambda: sent_rows(3, inner_ref))
+    for load in loads:
+        load.wait()
+    own_rows(1, 1)
+    own_rows(2, 0)
+    when(first_row, lambda: own_rows(0, 0))
+    when(last_row, lambda: own_rows(3, 1))
+
+    def repeat(target, source):
+        half_high[:, target] = half_high[:, source]
+        half_low[:, target] = half_low[:, source]
+
+    when(same(p.c, 0), lambda: repeat(low, pl.ds(PAIR, PAIR)))
+    when(same(p.c, GROUPS - 1), lambda: repeat(high, pl.ds(COLS, PAIR)))
     stores = []
     for slots, panel in SLOTS:
         columns = pl.ds(panel * PAIR, PAIR)
@@ -638,20 +623,18 @@
 
 
 def apply(matrix, parts):
-    any_spec = pl.BlockSpec(memory_space=pltpu.HBM)
+    hbm = pl.BlockSpec(memory_space=pltpu.HBM)
+    vmem = pl.BlockSpec(memory_space=pltpu.VMEM)
     return pl.pallas_call(
         apply_kernel,
         out_shape=jax.ShapeDtypeStruct((ROWS, COLS), F32),
-        in_specs=[any_spec] * 7,
-        out_specs=any_spec,
+        in_specs=[hbm] + [vmem] * 6,
+        out_specs=pl.BlockSpec(memory_space=pl.ANY),
         scratch_shapes=[
-            pltpu.VMEM((4, PAIR, WIDE), F32),
-            pltpu.VMEM((8, PAIR, BLK), F32),
-            pltpu.VMEM((4, BLK, PAIR), F32),
+            pltpu.VMEM((ROWS, COLS), F32),
             pltpu.VMEM((ROWS, WIDE), BF16),
             pltpu.VMEM((ROWS, WIDE), BF16),
             pltpu.VMEM((8, ROWS, BLK), F32),
-            pltpu.SemaphoreType.DMA((4, 3)),
             pltpu.SemaphoreType.DMA((2,)),
             pltpu.SemaphoreType.DMA((8,)),
         ],

time: 60.6 us -> 59.6 us (0.983)
  Pallas kernels: 60.4 us -> 59.4 us
    pallas_call x1, Pallas kernels: 5.49 us -> 4.49 us  [apply(): pl.pallas_call(apply_kernel, out_shape=jax.ShapeDtypeStruct((ROWS, COLS),...]
where the time goes in v5:
time: 59.6 us; the launch traced here: 59.4 us
  Pallas kernels  59.4 us (100%)
    pallas_call x1, Pallas kernels, travel(): pl.pallas_call(travel_kernel, out_shape=[pltpu.VMEM(shape, F32) for shape...  54 us
    pallas_call x1, Pallas kernels, apply(): pl.pallas_call(apply_kernel, out_shape=jax.ShapeDtypeStruct((ROWS, COLS),...  4.49 us

profile of v5, /device:TPU:79, one launch (start us, length us, event | category | flops | bytes accessed | tf_op | source)
XLA Modules:
  0.0 59.4 jit_solution(17386843901366643439)
XLA Ops:
  0.0 0.9 %first.1.first_ref = f32[264,128]{1,0:T(8,128)S(1)} custom-call(f32[512,1024]{1,0:T(8,128)} %m_ref.5), custom_call_target="tpu_custom_call" | custom-call | flops 1000000 | bytes 1000000 | tf_op jit(solution)/shard_map/first/pallas_call | solution.py:504
  0.9 54.0 %travel.1 = (f32[512,256]{1,0:T(8,128)S(1)}, f32[512,256]{1,0:T(8,128)S(1)}, f32[256,1536]{1,0:T(8,128)S(1)}, f32[256,1536]{1,0:T(8,128)S(1)}, f32[8,256,128]{2,1,0:T(8,128)S(1)}, /*index=5*/f32[4,128,256]{2,1,0:T(8,128)S(1)}) custom-call(f32[512,1024]{1,0:T(8,128)} %m_ref.5, f32[264,128]{1,0:T(8,128)S(1)} %first.1.first_ref), custom_call_target="tpu_custom_call" | custom-call | flops 1000000000 | bytes 10000000 | tf_op jit(solution)/shard_map/travel/pallas_call | solution.py:526
  55.0 4.5 %apply.1 = f32[512,1024]{1,0:T(8,128)} custom-call(f32[512,1024]{1,0:T(8,128)} %m_ref.5, f32[512,256]{1,0:T(8,128)S(1)} %get-tuple-element.11.left_ref, f32[512,256]{1,0:T(8,128)S(1)} %get-tuple-element.12.right_ref, f32[256,1536]{1,0:T(8,128)S(1)} %get-tuple-element.13.outer_ref, f32[256,1536]{1,0:T(8,128)S(1)} %get-tuple-element.14.inner_ref, ...), custom_call_target="tpu_custom_call" | custom-call | flops 2000000000 | bytes 10000000 | tf_op jit(solution)/shard_map/apply/pallas_call | solution.py:628

commit v6 on v5

--- a/solution.py
+++ b/solution.py
@@ -417,13 +417,13 @@
         arrived(side_pass.at[side], side_pass_sem.at[side], cond)
         part = pl.ds(pl.multiple_of(p.y * BLK, BLK), BLK)
         sends.start(cond, side_pass.at[side], sides[side].at[part], side_sem.at[side, p.y], device)
+
+    arrived(solver_in, solver_sem.at[0], 1 - p.in_relay)
     relaying, relay_to, _ = relay_role(p)
     arrived(relay, relay_sem.at[0], relaying)
     sends.start(
         relaying, relay, outer_ref.at[:, pl.ds(pl.multiple_of(PAIR + p.x * PAIR, PAIR), PAIR)], outer_sem.at[p.x], relay_to
     )
-
-    arrived(solver_in, solver_sem.at[0], 1 - p.in_relay)
     rotation = pair_rotation(unfold(jnp.where(p.in_relay == 1, first_ref[...], solver_in[...])))
 
     def keep_columns():

time: 59.6 us -> 59 us (0.990)
  the two profiles are of different devices: /device:TPU:79 before, /device:TPU:175 now
where the time goes in v6:
time: 59 us; the launch traced here: 58.8 us
  Pallas kernels  58.8 us (100%)
    pallas_call x1, Pallas kernels, travel(): pl.pallas_call(travel_kernel, out_shape=[pltpu.VMEM(shape, F32) for shape...  45.9 us
    pallas_call x1, Pallas kernels, first(): pl.pallas_call(first_kernel, out_shape=pltpu.VMEM((FOLD, BLK), F32), in_s...  8.4 us
    pallas_call x1, Pallas kernels, apply(): pl.pallas_call(apply_kernel, out_shape=jax.ShapeDtypeStruct((ROWS, COLS),...  4.49 us

profile of v6, /device:TPU:175, one launch (start us, length us, event | category | flops | bytes accessed | tf_op | source)
XLA Modules:
  0.0 58.8 jit_solution(14217339271662694186)
XLA Ops:
  0.0 8.4 %first.1.first_ref = f32[264,128]{1,0:T(8,128)S(1)} custom-call(f32[512,1024]{1,0:T(8,128)} %m_ref.5), custom_call_target="tpu_custom_call" | custom-call | flops 1000000 | bytes 1000000 | tf_op jit(solution)/shard_map/first/pallas_call | solution.py:504
  8.4 45.9 %travel.1 = (f32[512,256]{1,0:T(8,128)S(1)}, f32[512,256]{1,0:T(8,128)S(1)}, f32[256,1536]{1,0:T(8,128)S(1)}, f32[256,1536]{1,0:T(8,128)S(1)}, f32[8,256,128]{2,1,0:T(8,128)S(1)}, /*index=5*/f32[4,128,256]{2,1,0:T(8,128)S(1)}) custom-call(f32[512,1024]{1,0:T(8,128)} %m_ref.5, f32[264,128]{1,0:T(8,128)S(1)} %first.1.first_ref), custom_call_target="tpu_custom_call" | custom-call | flops 1000000000 | bytes 10000000 | tf_op jit(solution)/shard_map/travel/pallas_call | solution.py:526
  54.3 4.5 %apply.1 = f32[512,1024]{1,0:T(8,128)} custom-call(f32[512,1024]{1,0:T(8,128)} %m_ref.5, f32[512,256]{1,0:T(8,128)S(1)} %get-tuple-element.11.left_ref, f32[512,256]{1,0:T(8,128)S(1)} %get-tuple-element.12.right_ref, f32[256,1536]{1,0:T(8,128)S(1)} %get-tuple-element.13.outer_ref, f32[256,1536]{1,0:T(8,128)S(1)} %get-tuple-element.14.inner_ref, ...), custom_call_target="tpu_custom_call" | custom-call | flops 2000000000 | bytes 10000000 | tf_op jit(solution)/shard_map/apply/pallas_call | solution.py:628
